TPU v7x, 128 devices: a whole 4x4x4 slice. The times are simulated.
128 devices in a mesh: scan: 8 (over y, core), morton: 16 (over x, z).
Axes of the slice: x: 4, y: 4, z: 4, core: 2. Of those that a mesh axis runs over, the one named last changes fastest.
Arguments:
- positions: float32 [2048, 3, 128], P(('scan', 'morton')), may hold values from 0 to 7
- normals: float32 [2048, 3, 128], P(('scan', 'morton')), may hold values from -4 to 4
- weights: float32 [2048, 128], P(('scan', 'morton')), may hold values from 0.1 to 1
- point_target: int32 [2048], P(('scan', 'morton')), may hold values from 0 to 1023, as said below
- neighbours: int32 [1024, 27], P(('scan', 'morton')), may hold values from -1 to 1023, as said below
Outputs:
- solution_field: float32 [1024, 512], P(('scan', 'morton'))
- residual: float32 [1024, 512], P(('scan', 'morton'))
Inputs may be any that keep to these rules, and one draw needn't show every extreme that they name: point_target[q] // 8 % 16 equals (q // 16) % 16; of the 16 point blocks of one device, at most 4 have the same point_target // (16 * 8), and exactly 4 for some value on every device. `neighbours`: entry 9 (a + 1) + 3 (b + 1) + (c + 1) of a block's row names the block across offset (a, b, c); the centre entry is the block itself; if block g names h at an offset, h names g at the opposite offset; a named block h of row g satisfies |h // 8 - g // 8| <= 1.
All inputs are finite; a program needn't handle non-finite values.
Results may differ from a plain program's by a relative error of at most 0.0003.
Values sent between devices are 32-bit elements; how exact they have to be, the bound alone decides.
No kernel may reach another device: no remote copies, remote signals or barrier semaphores. Data moves between devices by JAX's collectives and lax.ppermute only.
A program may use at most 128 MiB of HBM per device.

v0:
```python
import math

import jax
import jax.numpy as jnp
import numpy as np
from jax import lax
from jax.sharding import PartitionSpec as P

ITERS = 2


SCREEN = 16.0


def padded(cells, sides, width):
    for axis, dim in sides:
        count = lax.axis_size(axis)
        ends = count - 1
        head = lax.slice_in_dim(cells, 0, width, axis=dim)
        tail = lax.slice_in_dim(cells, cells.shape[dim] - width, cells.shape[dim], axis=dim)
        cells = jnp.concatenate(
            [
                lax.ppermute(tail, axis, [(i, (i + 1) % count) for i in range(ends)]),
                cells,
                lax.ppermute(head, axis, [((i + 1) % count, i) for i in range(ends)]),
            ],
            axis=dim,
        )
    return cells


def splat(positions, normals, weights):
    count = positions.shape[0]
    group = math.gcd(count, 16)

    def one(pack):
        spots, norms, wts = pack
        nodes = jnp.arange(8).astype(spots.dtype)
        diff = spots[:, :, None, :] - nodes[None, None, :, None]
        dist = jnp.abs(diff)
        hat = jnp.maximum(0.0, 1.0 - dist)
        slope = jnp.where(dist < 1.0, -jnp.sign(diff), 0.0)
        points = spots.shape[-1]
        wn = wts[:, None, :]
        left = jnp.stack([wn * norms[:, 0, None, :] * slope[:, 0], wn * hat[:, 0]], axis=1)
        first = (hat[:, 1, :, None, :] * hat[:, 2, None, :, :]).reshape(group, 64, points)
        second = (
            norms[:, 1, None, None, :] * slope[:, 1, :, None, :] * hat[:, 2, None, :, :]
            + norms[:, 2, None, None, :] * hat[:, 1, :, None, :] * slope[:, 2, None, :, :]
        ).reshape(group, 64, points)
        right = jnp.stack([first, second], axis=1)
        rhs = jnp.einsum("gtip,gtmp->gim", left, right, precision=lax.Precision.HIGHEST)
        squares = hat * hat
        outer = (squares[:, 1, :, None, :] * squares[:, 2, None, :, :]).reshape(group, 64, points)
        scr = SCREEN * jnp.einsum(
            "gip,gmp->gim", wn * squares[:, 0], outer, precision=lax.Precision.HIGHEST
        )
        return (rhs.reshape(group, 512), scr.reshape(group, 512))

    packs = (
        positions.reshape(count // group, group, 3, -1),
        normals.reshape(count // group, group, 3, -1),
        weights.reshape(count // group, group, -1),
    )
    rhs, scr = lax.map(one, packs)
    return jnp.concatenate([rhs.reshape(count, 512), scr.reshape(count, 512)], axis=1)


def coefficient(a, b, c):
    mass = {-1: 1.0 / 6.0, 0: 2.0 / 3.0, 1: 1.0 / 6.0}
    stiff = {-1: -1.0, 0: 2.0, 1: -1.0}
    return (
        stiff[a] * mass[b] * mass[c] + mass[a] * stiff[b] * mass[c] + mass[a] * mass[b] * stiff[c]
    )


def crossing(spot):
    if spot < 0:
        return -1
    if spot > 7:
        return 1
    return 0


def coupling_table():
    table = np.zeros((27 * 512, 512), np.float32)
    for target in range(512):
        first, second, third = (target // 64, target // 8 % 8, target % 8)
        for a in (-1, 0, 1):
            for b in (-1, 0, 1):
                for c in (-1, 0, 1):
                    weight = coefficient(a, b, c)
                    if weight == 0.0:
                        continue
                    near_a, near_b, near_c = (first + a, second + b, third + c)
                    offset = (
                        (crossing(near_a) + 1) * 9
                        + (crossing(near_b) + 1) * 3
                        + (crossing(near_c) + 1)
                    )
                    source = near_a % 8 * 64 + near_b % 8 * 8 + near_c % 8
                    table[offset * 512 + source, target] += weight
    return table


def squares(current):
    return lax.psum(jnp.sum(current * current), ("scan", "morton"))


def per_device(positions, normals, weights, point_target, neighbours):
    blocks = neighbours.shape[0]
    n_morton = lax.axis_size("morton")
    owner = lax.axis_index("scan") * n_morton + lax.axis_index("morton")
    parts = splat(positions, normals, weights)
    column = point_target // (n_morton * blocks) * blocks + point_target % blocks
    rows = jnp.arange(lax.axis_size("scan") * blocks, dtype=jnp.int32)
    picks = (rows[:, None] == column[None, :]).astype(jnp.float32)
    fields = lax.psum_scatter(
        jnp.dot(picks, parts, precision=lax.Precision.HIGHEST, preferred_element_type=jnp.float32),
        "scan",
        scatter_dimension=0,
        tiled=True,
    )
    rhs = fields[:, :512]
    screen = fields[:, 512:]
    local = jnp.where(neighbours >= 0, neighbours - (owner - 1) * blocks, 3 * blocks)
    couplings = jnp.asarray(coupling_table())
    solution_field = jnp.zeros_like(rhs)
    residual = rhs
    direction = rhs
    norm_now = squares(residual)
    for step in range(ITERS):
        wide = padded(direction, ((("scan", "morton"), 0),), blocks)
        table = jnp.concatenate([wide, jnp.zeros((1, 512), direction.dtype)], axis=0)
        nearby = table[local].reshape(blocks, 27 * 512)
        image = screen * direction + jnp.dot(
            nearby, couplings, precision=lax.Precision.HIGHEST, preferred_element_type=jnp.float32
        )
        alpha = norm_now / lax.psum(jnp.sum(direction * image), ("scan", "morton"))
        solution_field = solution_field + alpha * direction
        residual = residual - alpha * image
        norm_next = squares(residual)
        direction = residual + norm_next / norm_now * direction
        norm_now = norm_next
    return (solution_field, residual)


def solution(mesh):
    placed = (
        P(("scan", "morton"), None, None),
        P(("scan", "morton"), None, None),
        P(("scan", "morton"), None),
        P(("scan", "morton")),
        P(("scan", "morton"), None),
    )
    return jax.shard_map(
        per_device,
        mesh=mesh,
        in_specs=placed,
        out_specs=(P(("scan", "morton"), None), P(("scan", "morton"), None)),
        check_vma=False,
    )
```

profile of v0, /device:TPU:1, one launch (start us, length us, event | category | flops | bytes accessed | tf_op | source)
XLA Modules:
  0.0 312.8 jit_solution(11254280374817374153)
XLA Ops:
  7.2 0.0 reduce-scatter.2.cloned.1.call-start
  7.2 0.8 copy.8
  8.0 0.2 fusion.9
  8.2 1.6 convolution_multiply_fusion
  9.8 0.1 reshape.144
  9.9 0.8 fusion.25
  10.6 0.7 slice_multiply_fusion
  11.4 0.1 multiply_bitcast_fusion
  11.5 1.0 convolution_bitcast_fusion
  12.5 0.1 reshape.143
  12.6 0.7 fusion.26
  13.2 0.9 fusion.18
  14.2 0.0 reduce-scatter.2.cloned.1.call-update
  14.2 0.7 compare_select_fusion
  14.9 0.1 reshape.149
  15.0 30.4 %reduce-scatter.2.cloned.1.call-done = f32[8,1024]{1,0:T(8,128)} async-done(((f32[64,1024]{1,0:T(8,128)}), f32[8,1024]{1,0:T(8,128)}) %reduce-scatter.2.cloned.1.call-update) | async-done | bytes 32784 | tf_op jit(solution)/shard_map/reduce_scatter | solution.py:118
  45.4 0.0 copy-start
  45.4 0.8 slice.83
  46.2 10.0 %collective-permute-start.1 = (f32[8,512]{1,0:T(8,128)S(1)}, f32[8,512]{1,0:T(8,128)S(1)}, u32[]{:S(2)}, u32[]{:S(2)}) collective-permute-start(f32[8,512]{1,0:T(8,128)S(1)} %slice.83), channel_id=1, source_target_pairs={{1,0},{2,1},{3,2},{4,3},{5,4},{6,5},{7,6},{8,7},{9,8},{10,9},{11,1... | collective-permute-start | bytes 49160 | tf_op jit(solution)/shard_map/ppermute | solution.py:25
  56.2 1.9 collective-permute-start
  58.1 0.1 pad.7.clone
  58.2 0.0 collective-permute-done.1
  58.2 6.4 %collective-permute-done = f32[8,512]{1,0:T(8,128)S(1)} collective-permute-done((f32[8,512]{1,0:T(8,128)S(1)}, f32[8,512]{1,0:T(8,128)S(1)}, u32[]{:S(2)}, u32[]{:S(2)}) %collective-permute-start) | collective-permute-done | bytes 16416 | tf_op jit(solution)/shard_map/ppermute | solution.py:23
  64.5 0.1 maximum_maximum_fusion
  64.6 0.9 gather_fusion
  65.5 0.2 reshape.145
  65.7 17.9 %multiply_reduce_fusion.2 = (f32[]{:T(128)}, f32[]{:T(128)}, f32[8,512]{1,0:T(8,128)S(1)}) fusion(f32[8,1024]{1,0:T(8,128)} %reduce-scatter.2.cloned.1.call-done, f32[8,13824]{1,0:T(8,128)S(1)} %reshape.145, f32[13824,512]{1,0:T(8,128)} %constant.76.clone), kind=kOutput, calls=%fused_computation.52 | convolution fusion | flops 679501824 | bytes 28803080 | tf_op jit(solution)/shard_map/dot_general | solution.py:136
  83.7 61.8 %all-reduce = (f32[]{:T(128)}, f32[]{:T(128)}) all-reduce(f32[]{:T(128)} %get-tuple-element.15, f32[]{:T(128)} %get-tuple-element.14), channel_id=1, replica_groups=mesh['scan'=8,'morton'=16] {'scan','morton'}, use_global_device_ids=true, to_apply=%region_2.3 | all-reduce | flops 2 | bytes 16 | tf_op jit(solution)/shard_map/psum | solution.py:107
  146.9 0.0 copy-done
  146.9 0.6 multiply_reduce_fusion.1
  147.5 63.4 %psum.30 = f32[]{:T(128)} all-reduce(f32[]{:T(128)} %multiply_reduce_fusion.1), channel_id=1, replica_groups=mesh['scan'=8,'morton'=16] {'scan','morton'}, use_global_device_ids=true, to_apply=%region_6.7 | all-reduce | flops 1 | bytes 8 | tf_op jit(solution)/shard_map/psum | solution.py:107
  212.2 4.8 %collective-permute-start.3 = (f32[8,512]{1,0:T(8,128)S(1)}, f32[8,512]{1,0:T(8,128)S(1)}, u32[]{:S(2)}, u32[]{:S(2)}) collective-permute-start(f32[8,512]{1,0:T(8,128)S(1)} %multiply_add_fusion.1), channel_id=1, source_target_pairs={{1,0},{2,1},{3,2},{4,3},{5,4},{6,5},{7,6},{8,7},{9,8},{10,9},{11,1... | collective-permute-start | bytes 49160 | tf_op jit(solution)/shard_map/ppermute | solution.py:25
  217.0 2.1 collective-permute-start.2
  219.1 0.0 collective-permute-done.3
  219.2 6.4 %collective-permute-done.2 = f32[8,512]{1,0:T(8,128)S(1)} collective-permute-done((f32[8,512]{1,0:T(8,128)S(1)}, f32[8,512]{1,0:T(8,128)S(1)}, u32[]{:S(2)}, u32[]{:S(2)}) %collective-permute-start.2) | collective-permute-done | bytes 16416 | tf_op jit(solution)/shard_map/ppermute | solution.py:23
  225.5 0.1 maximum_maximum_fusion.1
  225.6 0.9 gather_fusion.1
  226.5 0.2 reshape.146
  226.7 15.3 %multiply_reduce_fusion = (f32[]{:T(128)}, f32[8,512]{1,0:T(8,128)S(1)}) fusion(f32[8,512]{1,0:T(8,128)S(1)} %multiply_add_fusion.1, f32[8,13824]{1,0:T(8,128)S(1)} %reshape.146, f32[13824,512]{1,0:T(8,128)} %constant.76.clone, f32[8,1024]{1,0:T(8,128)S(1)} %copy-done), kind=kOutput, calls=%fused_computation.48 | convolution fusion | flops 679493632 | bytes 28803076 | tf_op jit(solution)/shard_map/dot_general | solution.py:136
  242.0 62.0 %psum.31 = f32[]{:T(128)} all-reduce(f32[]{:T(128)} %get-tuple-element.42), channel_id=1, replica_groups=mesh['scan'=8,'morton'=16] {'scan','morton'}, use_global_device_ids=true, to_apply=%region_8.9 | all-reduce | flops 1 | bytes 8 | tf_op jit(solution)/shard_map/psum | solution.py:139
  305.3 0.6 multiply_subtract_fusion
  (5 shorter events, 0.0 us)
Async XLA Ops:
  7.2 38.2 %reduce-scatter.2.cloned.1.call-start = ((), (), s32[]{:S(2)}) async-start(), calls=%async_computation.1 | async-start | bytes 294912 | tf_op jit(solution)/shard_map/reduce_scatter | solution.py:118
  45.4 101.5 %copy-start = (f32[8,1024]{1,0:T(8,128)S(1)}, f32[8,1024]{1,0:T(8,128)}, u32[]{:S(2)}) copy-start(f32[8,1024]{1,0:T(8,128)} %reduce-scatter.2.cloned.1.call-done) | copy-start | bytes 98308
  46.2 12.0 %collective-permute-start.1 = (f32[8,512]{1,0:T(8,128)S(1)}, f32[8,512]{1,0:T(8,128)S(1)}, u32[]{:S(2)}, u32[]{:S(2)}) collective-permute-start(f32[8,512]{1,0:T(8,128)S(1)} %slice.83), channel_id=1, source_target_pairs={{1,0},{2,1},{3,2},{4,3},{5,4},{6,5},{7,6},{8,7},{9,8},{10,9},{11,1... | collective-permute-start | bytes 49160 | tf_op jit(solution)/shard_map/ppermute | solution.py:25
  56.2 8.4 %collective-permute-start = (f32[8,512]{1,0:T(8,128)S(1)}, f32[8,512]{1,0:T(8,128)S(1)}, u32[]{:S(2)}, u32[]{:S(2)}) collective-permute-start(f32[8,512]{1,0:T(8,128)S(1)} %slice.83), channel_id=1, source_target_pairs={{0,1},{1,2},{2,3},{3,4},{4,5},{5,6},{6,7},{7,8},{8,9},{9,10},{10,1... | collective-permute-start | bytes 49160 | tf_op jit(solution)/shard_map/ppermute | solution.py:23
  212.2 6.9 %collective-permute-start.3 = (f32[8,512]{1,0:T(8,128)S(1)}, f32[8,512]{1,0:T(8,128)S(1)}, u32[]{:S(2)}, u32[]{:S(2)}) collective-permute-start(f32[8,512]{1,0:T(8,128)S(1)} %multiply_add_fusion.1), channel_id=1, source_target_pairs={{1,0},{2,1},{3,2},{4,3},{5,4},{6,5},{7,6},{8,7},{9,8},{10,9},{11,1... | collective-permute-start | bytes 49160 | tf_op jit(solution)/shard_map/ppermute | solution.py:25
  217.0 8.5 %collective-permute-start.2 = (f32[8,512]{1,0:T(8,128)S(1)}, f32[8,512]{1,0:T(8,128)S(1)}, u32[]{:S(2)}, u32[]{:S(2)}) collective-permute-start(f32[8,512]{1,0:T(8,128)S(1)} %multiply_add_fusion.1), channel_id=1, source_target_pairs={{0,1},{1,2},{2,3},{3,4},{4,5},{5,6},{6,7},{7,8},{8,9},{9,10},{10,1... | collective-permute-start | bytes 49160 | tf_op jit(solution)/shard_map/ppermute | solution.py:23
Sparse Core Ops, SparseCore 0:
  14.3 31.0 reduce-scatter.1
where the time goes:
time: 314 us; the launch traced here: 313 us
  blocking collectives  187 us (60%)
  waiting for transfers between devices  43.1 us (14%)
  matrix products  36.8 us (12%)
  starting transfers between devices  18.8 us (6%)
  between operations  18.2 us (6%)
  other arithmetic  4.56 us (1%)
  local copies, waits for them, and re-layouts  4.14 us (1%)
    psum x2, blocking collectives, squares(): return lax.psum(jnp.sum(current * current), ('scan', 'morton'))  125 us
    psum x1, blocking collectives, per_device(): alpha = norm_now / lax.psum(jnp.sum(direction * image), ('scan', 'morton'))  62 us
    dot_general x2, matrix products, per_device(): jnp.dot(nearby, couplings, precision=lax.Precision.HIGHEST, preferred_ele...  33.2 us
    reduce_scatter x1, waiting for transfers between devices, per_device(): lax.psum_scatter(jnp.dot(picks, parts, precision=lax.Precision.HIGHEST, p...  30.4 us
    ppermute x2, starting transfers between devices, padded(): lax.ppermute(head, axis, [((i + 1) % count, i) for i in range(ends)])  14.8 us
    ppermute x2, waiting for transfers between devices, padded(): lax.ppermute(tail, axis, [(i, (i + 1) % count) for i in range(ends)])  12.7 us
  transfers between devices with their start and end apart: 5, of which 3 were waited for; matrix products, arithmetic and copies ran while one was open for 0% of the time, Pallas kernels for 0%

commit v1 on v0

v1 whole, which is shorter than its diff:
```python
import jax
import jax.numpy as jnp
import numpy as np
from jax import lax
from jax.experimental import pallas as pl
from jax.experimental.pallas import tpu as pltpu
from jax.sharding import PartitionSpec as P

SCREEN = 16.0
BLOCKS = 8
SLOTS = 4
SHARE = SLOTS * 8 + 8
BOTH = ("scan", "morton")


def plane_table():
    mass = {-1: 1.0, 0: 4.0, 1: 1.0}
    stiff = {-1: -1.0, 0: 2.0, 1: -1.0}
    table = np.zeros((640, 128), np.float32)
    for b in (-1, 0, 1):
        for c in (-1, 0, 1):
            for row in range(64):
                for col in range(64):
                    dj = 8 * b + row // 8 - col // 8
                    dk = 8 * c + row % 8 - col % 8
                    if abs(dj) > 1 or abs(dk) > 1:
                        continue
                    at = 64 * (3 * (b + 1) + (c + 1)) + row
                    table[at, col] = mass[dj] * mass[dk]
                    table[at, 64 + col] = stiff[dj] * mass[dk] + mass[dj] * stiff[dk]
    return table


def split(values):
    high = values.astype(jnp.bfloat16)
    low = (values - high.astype(jnp.float32)).astype(jnp.bfloat16)
    return high, low


def nt(left, right):
    return lax.dot_general(left, right, (((1,), (1,)), ((), ())), preferred_element_type=jnp.float32)


def left_half():
    return lax.broadcasted_iota(jnp.int32, (8, 128), 1) < 64


def splat_kernel(target_ref, spots_ref, norms_ref, weights_ref, out_ref, used_ref):
    node = lax.broadcasted_iota(jnp.int32, (8, 128), 0).astype(jnp.float32)
    first_half = left_half()
    nothing = jnp.zeros((64, 128), jnp.float32)
    for row in range(8):
        used_ref[row] = 0
        out_ref[row * SHARE + SLOTS * 8 : (row + 1) * SHARE, :] = jnp.full((8, 128), -1.0, jnp.float32)
    for q in range(16):
        hats, slopes = [], []
        for dim in range(3):
            diff = spots_ref[q, dim : dim + 1, :] - node
            dist = jnp.abs(diff)
            hats.append(jnp.maximum(0.0, 1.0 - dist))
            way = jnp.where(diff > 0.0, -1.0, jnp.where(diff < 0.0, 1.0, 0.0))
            slopes.append(jnp.where(dist < 1.0, way, 0.0))
        weight = weights_ref[q : q + 1, :]
        one = weight * norms_ref[q, 0:1, :] * slopes[0]
        two = weight * hats[0]
        three = SCREEN * two * hats[0]
        slope1 = norms_ref[q, 1:2, :] * slopes[1]
        slope2 = norms_ref[q, 2:3, :] * slopes[2]
        square1 = hats[1] * hats[1]
        square2 = hats[2] * hats[2]
        first = jnp.concatenate([hats[1][j : j + 1] * hats[2] for j in range(8)], axis=0)
        second = jnp.concatenate(
            [slope1[j : j + 1] * hats[2] + hats[1][j : j + 1] * slope2 for j in range(8)], axis=0
        )
        outer = jnp.concatenate([square1[j : j + 1] * square2 for j in range(8)], axis=0)
        right = jnp.concatenate(
            [jnp.concatenate([first, second], axis=1), jnp.concatenate([outer, nothing], axis=1)], axis=0
        )
        left = jnp.concatenate(
            [
                jnp.concatenate([one, two], axis=1),
                jnp.concatenate([three, jnp.zeros((8, 128), jnp.float32)], axis=1),
            ],
            axis=0,
        )
        right_high, right_low = split(right)
        left_high, left_low = split(left)
        main = nt(jnp.concatenate([left_high, left_low], axis=0), right_high)
        total = main[:16] + main[16:] + nt(left_high, right_low)
        target = target_ref[q]
        row = target // (16 * BLOCKS)
        slot = used_ref[row]
        used_ref[row] = slot + 1
        place = pl.multiple_of(row * SHARE + slot * 8, 8)
        out_ref[pl.ds(place, 8), :] = jnp.where(first_half, total[:8], total[8:])
        block = (target % BLOCKS).astype(jnp.float32)
        out_ref[pl.ds(row * SHARE + SLOTS * 8 + slot, 1), :] = jnp.full((1, 128), block, jnp.float32)


def combine_kernel(parts_ref, out_ref):
    sums = [jnp.zeros((8, 128), jnp.float32) for _ in range(BLOCKS)]
    for source in range(8):
        for slot in range(SLOTS):
            at = source * SHARE
            part = parts_ref[at + slot * 8 : at + slot * 8 + 8, :]
            name = jnp.broadcast_to(parts_ref[at + SLOTS * 8 + slot : at + SLOTS * 8 + slot + 1, :], (8, 128))
            for block in range(BLOCKS):
                sums[block] = sums[block] + jnp.where(name == float(block), part, 0.0)
    for block in range(BLOCKS):
        out_ref[block] = sums[block]


def doubled(tile, first_half):
    return jnp.where(first_half, tile, pltpu.roll(tile, 64, 1))


def couple(near_ref, wide_ref, planes_ref, rows_ref, table_ref):
    first_half = left_half()
    first_row = first_half[:1]
    me = lax.axis_index("scan") * lax.axis_size("morton") + lax.axis_index("morton")
    base = (me - 1) * BLOCKS

    def place(block, offset):
        named = near_ref[block, offset]
        return jnp.where(named < 0, 3 * BLOCKS, named - base)

    for block in range(BLOCKS):
        for pair in range(5):
            lanes = slice(128 * pair, 128 * pair + 128)
            for shift, plane, at in ((0, 7, 64 + block), (9, None, 8 * block), (18, 0, 72 + block)):
                rows = slice(0, 8) if plane is None else slice(plane, plane + 1)
                tile = wide_ref[place(block, shift + 2 * pair), rows, :]
                if pair < 4:
                    other = wide_ref[place(block, shift + 2 * pair + 1), rows, :]
                    tile = jnp.where(first_half if plane is None else first_row, tile, other)
                rows_ref[at : at + tile.shape[0], lanes] = tile
    high, low = split(rows_ref[...])
    both = jnp.dot(
        jnp.concatenate([high, low], axis=0), table_ref[...], preferred_element_type=jnp.float32
    )
    sums = both[:80] + both[80:]
    result = []
    centre = jnp.where(first_half, 2.0 / 36.0, 4.0 / 36.0)
    side = jnp.where(first_half, -1.0 / 36.0, 1.0 / 36.0)
    for block in range(BLOCKS):
        planes_ref[block, 1:9, :] = sums[8 * block : 8 * block + 8]
        planes_ref[block, 0:1, :] = sums[64 + block : 65 + block]
        planes_ref[block, 9:10, :] = sums[72 + block : 73 + block]
    for block in range(BLOCKS):
        around = planes_ref[block, 0:8, :] + planes_ref[block, 2:10, :]
        value = centre * sums[8 * block : 8 * block + 8] + side * around
        result.append(value + pltpu.roll(value, 64, 1))
    return result


def fill(wide_ref, own_ref, before_ref, after_ref, first_half):
    for block in range(BLOCKS):
        wide_ref[block] = doubled(before_ref[block], first_half)
        wide_ref[BLOCKS + block] = doubled(own_ref[block], first_half)
        wide_ref[2 * BLOCKS + block] = doubled(after_ref[block], first_half)
    wide_ref[3 * BLOCKS] = jnp.zeros((8, 128), jnp.float32)


def image_of(own_ref, before_ref, after_ref, fields_ref, near_ref, table_ref, wide_ref, rows_ref, planes_ref):
    first_half = left_half()
    fill(wide_ref, own_ref, before_ref, after_ref, first_half)
    coupled = couple(near_ref, wide_ref, planes_ref, rows_ref, table_ref)
    images = []
    for block in range(BLOCKS):
        tile = fields_ref[block]
        screen = jnp.where(first_half, pltpu.roll(tile, 64, 1), tile)
        images.append(screen * wide_ref[BLOCKS + block] + coupled[block])
    return images


def first_kernel(near_ref, fields_ref, before_ref, after_ref, table_ref, out_ref, wide_ref, rows_ref, planes_ref):
    images = image_of(
        fields_ref, before_ref, after_ref, fields_ref, near_ref, table_ref, wide_ref, rows_ref, planes_ref
    )
    for block in range(BLOCKS):
        out_ref[block] = images[block]


def total(lefts, rights, first_half):
    terms = [a * b for a, b in zip(lefts, rights)]
    while len(terms) > 1:
        terms = [a + b for a, b in zip(terms[::2], terms[1::2])]
    return jnp.sum(jnp.where(first_half, terms[0], 0.0), axis=(0, 1), keepdims=True)


def second_kernel(
    near_ref, own_ref, before_ref, after_ref, fields_ref, table_ref, out_ref, sums_ref, wide_ref, rows_ref, planes_ref
):
    second = image_of(
        own_ref, before_ref, after_ref, fields_ref, near_ref, table_ref, wide_ref, rows_ref, planes_ref
    )
    first_half = left_half()
    start = [fields_ref[block] for block in range(BLOCKS)]
    first = [own_ref[block] for block in range(BLOCKS)]
    lane = lax.broadcasted_iota(jnp.int32, (1, 128), 1)
    packed = jnp.zeros((1, 128), jnp.float32)
    pairs = ((start, start), (start, first), (first, first), (start, second), (first, second))
    for place, (a, b) in enumerate(pairs):
        packed = jnp.where(lane == place, total(a, b, first_half), packed)
    sums_ref[...] = jnp.broadcast_to(packed, (128, 128))
    for block in range(BLOCKS):
        out_ref[block] = second[block]


def last_kernel(sums_ref, fields_ref, first_ref, second_ref, solution_ref, residual_ref, left_ref, right_ref):
    first_half = left_half()
    sums = jnp.sum(sums_ref[...], axis=0, keepdims=True)
    lane = lax.broadcasted_iota(jnp.int32, (1, 128), 1)

    def pick(place):
        return jnp.sum(jnp.where(lane == place, sums, 0.0), axis=1, keepdims=True)

    s00, s01, s11, s02, s12 = (pick(place) for place in range(5))
    alpha0 = s00 / s01
    norm1 = s00 - 2.0 * alpha0 * s01 + alpha0 * alpha0 * s11
    beta = norm1 / s00
    grow = 1.0 + beta
    curve = grow * grow * s01 - grow * alpha0 * (s02 + s11) + alpha0 * alpha0 * s12
    alpha1 = norm1 / curve
    for block in range(BLOCKS):
        start = doubled(fields_ref[block], first_half)
        first = first_ref[block]
        left = start - alpha0 * first
        direction = left + beta * start
        image = grow * first - alpha0 * second_ref[block]
        left_ref[block] = alpha0 * start + alpha1 * direction
        right_ref[block] = left - alpha1 * image
    for pair in range(4):
        lanes = slice(128 * pair, 128 * pair + 128)
        solution_ref[:, lanes] = jnp.where(first_half, left_ref[:, 2 * pair, :], left_ref[:, 2 * pair + 1, :])
        residual_ref[:, lanes] = jnp.where(first_half, right_ref[:, 2 * pair, :], right_ref[:, 2 * pair + 1, :])


def vmem(count):
    return [pl.BlockSpec(memory_space=pltpu.VMEM)] * count


def smem(count):
    return [pl.BlockSpec(memory_space=pltpu.SMEM)] * count


def shape(*dims):
    return jax.ShapeDtypeStruct(dims, jnp.float32)


STENCIL_SCRATCH = [
    pltpu.VMEM((3 * BLOCKS + 1, 8, 128), jnp.float32),
    pltpu.VMEM((80, 640), jnp.float32),
    pltpu.VMEM((BLOCKS, 16, 128), jnp.float32),
]


def around(values):
    count = lax.axis_size("scan") * lax.axis_size("morton")
    up = [(i, i + 1) for i in range(count - 1)]
    down = [(i + 1, i) for i in range(count - 1)]
    return lax.ppermute(values, BOTH, up), lax.ppermute(values, BOTH, down)


def per_device(positions, normals, weights, point_target, neighbours):
    table = jnp.asarray(plane_table(), jnp.bfloat16)
    parts = pl.pallas_call(
        splat_kernel,
        out_shape=shape(8 * SHARE, 128),
        in_specs=smem(1) + vmem(3),
        out_specs=vmem(1)[0],
        scratch_shapes=[pltpu.SMEM((8,), jnp.int32)],
        name="splat",
    )(point_target, positions, normals, weights)
    parts = lax.all_to_all(parts, "scan", 0, 0, tiled=True)
    fields = pl.pallas_call(
        combine_kernel, out_shape=shape(BLOCKS, 8, 128), in_specs=vmem(1), out_specs=vmem(1)[0], name="combine"
    )(parts)
    before, after = around(fields)
    first = pl.pallas_call(
        first_kernel,
        out_shape=shape(BLOCKS, 8, 128),
        in_specs=smem(1) + vmem(4),
        out_specs=vmem(1)[0],
        scratch_shapes=STENCIL_SCRATCH,
        name="first",
    )(neighbours, fields, before, after, table)
    before, after = around(first)
    second, sums = pl.pallas_call(
        second_kernel,
        out_shape=(shape(BLOCKS, 8, 128), shape(128, 128)),
        in_specs=smem(1) + vmem(5),
        out_specs=tuple(vmem(2)),
        scratch_shapes=STENCIL_SCRATCH,
        name="second",
    )(neighbours, first, before, after, fields, table)
    sums = lax.all_to_all(sums, BOTH, 0, 0, tiled=True)
    return pl.pallas_call(
        last_kernel,
        out_shape=(shape(BLOCKS, 512), shape(BLOCKS, 512)),
        in_specs=vmem(4),
        out_specs=tuple(vmem(2)),
        scratch_shapes=[pltpu.VMEM((BLOCKS, 8, 128), jnp.float32)] * 2,
        name="last",
    )(sums, fields, first, second)


def solution(mesh):
    placed = (
        P(BOTH, None, None),
        P(BOTH, None, None),
        P(BOTH, None),
        P(BOTH),
        P(BOTH, None),
    )
    return jax.shard_map(
        per_device,
        mesh=mesh,
        in_specs=placed,
        out_specs=(P(BOTH, None), P(BOTH, None)),
        check_vma=False,
    )
```

time: 314 us -> 68.5 us (0.22)
  blocking collectives: 187 us -> 25.8 us
  matrix products: 36.8 us -> 0 us
  waiting for transfers between devices: 43.1 us -> 12.4 us
  between operations: 18.2 us -> 0.71 us
  Pallas kernels: 0 us -> 10 us
  other arithmetic: 4.56 us -> 0 us
    psum x3 -> x0, blocking collectives: 187 us -> none  [the longest x2 125 us: squares(): return lax.psum(jnp.sum(current * current), ('scan', 'morton'))]
    dot_general x5 -> x0, matrix products: 36.8 us -> none  [the longest x2 33.2 us: per_device(): jnp.dot(nearby, couplings, precision=lax.Precision.HIGHEST, preferred_ele...]
    reduce_scatter x1 -> x0, waiting for transfers between devices: 30.4 us -> none  [per_device(): lax.psum_scatter(jnp.dot(picks, parts, precision=lax.Precision.HIGHEST, p...]
    all_to_all x0 -> x2, blocking collectives: none -> 25.8 us  [the longest x1 14.2 us: per_device(): sums = lax.all_to_all(sums, BOTH, 0, 0, tiled=True)]
    pallas_call x0 -> x5, Pallas kernels: none -> 10 us  [the longest x1 2.36 us: per_device(): pl.pallas_call(second_kernel, out_shape=(shape(BLOCKS, 8, 128), shape(128...]
  transfers between devices with their start and end apart: 5 -> 4, of which waited for: 3 -> 2; matrix products, arithmetic and copies ran while one was open for 0% -> 0% of each run, Pallas kernels for 0% -> 0%
where the time goes in v1:
time: 68.5 us; the launch traced here: 68 us
  blocking collectives  25.8 us (38%)
  starting transfers between devices  15.8 us (23%)
  waiting for transfers between devices  12.4 us (18%)
  Pallas kernels  10 us (15%)
  local copies, waits for them, and re-layouts  3.21 us (5%)
  between operations  0.71 us (1%)
    ppermute x4, starting transfers between devices, around(): return (lax.ppermute(values, BOTH, up), lax.ppermute(values, BOTH, down))  15.8 us
    all_to_all x1, blocking collectives, per_device(): sums = lax.all_to_all(sums, BOTH, 0, 0, tiled=True)  14.2 us
    ppermute x4, waiting for transfers between devices, around(): return (lax.ppermute(values, BOTH, up), lax.ppermute(values, BOTH, down))  12.4 us
    all_to_all x1, blocking collectives, per_device(): parts = lax.all_to_all(parts, 'scan', 0, 0, tiled=True)  11.7 us
    unnamed x12, local copies, waits for them, and re-layouts  3.21 us
    pallas_call x1, Pallas kernels, per_device(): pl.pallas_call(second_kernel, out_shape=(shape(BLOCKS, 8, 128), shape(128...  2.36 us
    pallas_call x1, Pallas kernels, per_device(): pl.pallas_call(first_kernel, out_shape=shape(BLOCKS, 8, 128), in_specs=sm...  2.2 us
    pallas_call x1, Pallas kernels, per_device(): pl.pallas_call(splat_kernel, out_shape=shape(8 * SHARE, 128), in_specs=sm...  2.17 us
  transfers between devices with their start and end apart: 4, of which 2 were waited for; matrix products, arithmetic and copies ran while one was open for 0% of the time, Pallas kernels for 0%

profile of v1, /device:TPU:1, one launch (start us, length us, event | category | flops | bytes accessed | tf_op | source)
XLA Modules:
  0.0 68.0 jit_solution(1135479287013417262)
XLA Ops:
  0.6 0.0 copy-start.4
  0.6 1.4 %copy.10.spots_ref = f32[16,3,128]{2,1,0:T(4,128)} copy(f32[16,3,128]{2,0,1:T(8,128)} %param.6) | data formatting | bytes 49152 | tf_op args[0]
  2.0 0.0 copy-done.4
  2.0 0.6 copy.11.norms_ref
  2.6 2.2 %splat.1 = f32[320,128]{1,0:T(8,128)} custom-call(s32[16]{0:T(128)} %target_ref.1, f32[16,3,128]{2,1,0:T(4,128)} %copy.10.spots_ref, f32[16,3,128]{2,1,0:T(4,128)} %copy.11.norms_ref, f32[16,128]{1,0:T(8,128)} %weights_ref.1), custom_call_target="tpu_custom_call" | custom-call | tf_op jit(solution)/shard_map/splat/pallas_call | solution.py:267
  4.8 11.7 %all_to_all.22 = f32[8,40,128]{2,1,0:T(8,128)} all-to-all(f32[8,40,128]{2,1,0:T(8,128)} %bitcast.6), channel_id=1, replica_groups=mesh['scan'=8,'morton'=16] {'scan'}, dimensions={0} | all-to-all | bytes 327680 | tf_op jit(solution)/shard_map/all_to_all | solution.py:275
  16.5 1.6 %combine.1.fields_ref = f32[8,8,128]{2,1,0:T(8,128)} custom-call(f32[320,128]{1,0:T(8,128)} %bitcast.7), custom_call_target="tpu_custom_call" | custom-call | tf_op jit(solution)/shard_map/combine/pallas_call | solution.py:276
  18.1 8.6 %collective-permute-start.1 = (f32[8,8,128]{2,1,0:T(8,128)}, f32[8,8,128]{2,1,0:T(8,128)S(1)}, u32[]{:S(2)}, u32[]{:S(2)}) collective-permute-start(f32[8,8,128]{2,1,0:T(8,128)} %combine.1.fields_ref), channel_id=1, source_target_pairs={{1,0},{2,1},{3,2},{4,3},{5,4},{6,5},{7,6},{8,7},{9,8},{10,9},{11,1... | collective-permute-start | bytes 98312 | tf_op jit(solution)/shard_map/ppermute | solution.py:262
  26.7 1.9 %collective-permute-start = (f32[8,8,128]{2,1,0:T(8,128)}, f32[8,8,128]{2,1,0:T(8,128)S(1)}, u32[]{:S(2)}, u32[]{:S(2)}) collective-permute-start(f32[8,8,128]{2,1,0:T(8,128)} %combine.1.fields_ref), channel_id=1, source_target_pairs={{0,1},{1,2},{2,3},{3,4},{4,5},{5,6},{6,7},{7,8},{8,9},{9,10},{10,1... | collective-permute-start | bytes 98312 | tf_op jit(solution)/shard_map/ppermute | solution.py:262
  28.7 0.0 collective-permute-done.1.after_ref
  28.7 0.0 copy-start.1
  28.7 7.0 %collective-permute-done.before_ref = f32[8,8,128]{2,1,0:T(8,128)S(1)} collective-permute-done((f32[8,8,128]{2,1,0:T(8,128)}, f32[8,8,128]{2,1,0:T(8,128)S(1)}, u32[]{:S(2)}, u32[]{:S(2)}) %collective-permute-start) | collective-permute-done | bytes 32800 | tf_op jit(solution)/shard_map/ppermute | solution.py:262
  35.7 0.0 copy-done.1
  35.7 0.0 copy-start.3
  35.7 0.6 copy-done.3
  36.3 2.2 %first.1.own_ref.first_ref = f32[8,8,128]{2,1,0:T(8,128)} custom-call(s32[8,27]{1,0:T(8,128)} %near_ref.3, f32[8,8,128]{2,1,0:T(8,128)} %combine.1.fields_ref, f32[8,8,128]{2,1,0:T(8,128)} %copy-done.3, f32[8,8,128]{2,1,0:T(8,128)} %copy-done.1, bf16[640,128]{1,0:T(8,128)(2,1)} %constant.2.clone.table_ref), custom_call_target="tpu_custom_call" | custom-call | tf_op jit(solution)/shard_map/first/pallas_call | solution.py:280
  38.5 1.9 %collective-permute-start.3 = (f32[8,8,128]{2,1,0:T(8,128)}, f32[8,8,128]{2,1,0:T(8,128)S(1)}, u32[]{:S(2)}, u32[]{:S(2)}) collective-permute-start(f32[8,8,128]{2,1,0:T(8,128)} %first.1.own_ref.first_ref), channel_id=1, source_target_pairs={{1,0},{2,1},{3,2},{4,3},{5,4},{6,5},{7,6},{8,7},{9,8},{10,9},{11,1... | collective-permute-start | bytes 98312 | tf_op jit(solution)/shard_map/ppermute | solution.py:262
  40.4 3.4 %collective-permute-start.2 = (f32[8,8,128]{2,1,0:T(8,128)}, f32[8,8,128]{2,1,0:T(8,128)S(1)}, u32[]{:S(2)}, u32[]{:S(2)}) collective-permute-start(f32[8,8,128]{2,1,0:T(8,128)} %first.1.own_ref.first_ref), channel_id=1, source_target_pairs={{0,1},{1,2},{2,3},{3,4},{4,5},{5,6},{6,7},{7,8},{8,9},{9,10},{10,1... | collective-permute-start | bytes 98312 | tf_op jit(solution)/shard_map/ppermute | solution.py:262
  43.8 0.0 collective-permute-done.3.after_ref
  43.8 0.0 copy-start
  43.8 5.4 %collective-permute-done.2.before_ref = f32[8,8,128]{2,1,0:T(8,128)S(1)} collective-permute-done((f32[8,8,128]{2,1,0:T(8,128)}, f32[8,8,128]{2,1,0:T(8,128)S(1)}, u32[]{:S(2)}, u32[]{:S(2)}) %collective-permute-start.2) | collective-permute-done | bytes 32800 | tf_op jit(solution)/shard_map/ppermute | solution.py:262
  49.2 0.0 copy-done
  49.2 0.0 copy-start.2
  49.2 0.6 copy-done.2
  49.8 2.4 %second.1 = (f32[8,8,128]{2,1,0:T(8,128)}, f32[128,128]{1,0:T(8,128)}) custom-call(s32[8,27]{1,0:T(8,128)} %near_ref.3, f32[8,8,128]{2,1,0:T(8,128)} %first.1.own_ref.first_ref, f32[8,8,128]{2,1,0:T(8,128)} %copy-done.2, f32[8,8,128]{2,1,0:T(8,128)} %copy-done, f32[8,8,128]{2,1,0:T(8,128)} %combine.1.fields_ref, bf16[640,128]{1,0:T(8,128)(2,1)} %constant.2.clone.table_ref), custom_call_target="tpu_custom_call" | custom-call | tf_op jit(solution)/shard_map/second/pallas_call | solution.py:289
  52.1 14.2 %all_to_all.23 = f32[128,1,128]{2,1,0:T(1,128)} all-to-all(f32[128,1,128]{2,1,0:T(1,128)} %bitcast.9), channel_id=1, replica_groups=mesh['scan'=8,'morton'=16] {'scan','morton'}, dimensions={0} | all-to-all | bytes 131072 | tf_op jit(solution)/shard_map/all_to_all | solution.py:297
  66.3 1.7 %last.1 = (f32[8,512]{1,0:T(8,128)}, f32[8,512]{1,0:T(8,128)}) custom-call(f32[128,128]{1,0:T(8,128)} %bitcast.8, f32[8,8,128]{2,1,0:T(8,128)} %combine.1.fields_ref, f32[8,8,128]{2,1,0:T(8,128)} %first.1.own_ref.first_ref, f32[8,8,128]{2,1,0:T(8,128)} %get-tuple-element.5.second_ref), custom_call_target="tpu_custom_call" | custom-call | tf_op jit(solution)/shard_map/last/pallas_call | solution.py:298
Async XLA Ops:
  0.6 1.4 %copy-start.4 = (f32[16,3,128]{2,0,1:T(8,128)S(1)}, f32[16,3,128]{2,0,1:T(8,128)}, u32[]{:S(2)}) copy-start(f32[16,3,128]{2,0,1:T(8,128)} %param.7) | copy-start | bytes 73732
  18.1 10.6 %collective-permute-start.1 = (f32[8,8,128]{2,1,0:T(8,128)}, f32[8,8,128]{2,1,0:T(8,128)S(1)}, u32[]{:S(2)}, u32[]{:S(2)}) collective-permute-start(f32[8,8,128]{2,1,0:T(8,128)} %combine.1.fields_ref), channel_id=1, source_target_pairs={{1,0},{2,1},{3,2},{4,3},{5,4},{6,5},{7,6},{8,7},{9,8},{10,9},{11,1... | collective-permute-start | bytes 98312 | tf_op jit(solution)/shard_map/ppermute | solution.py:262
  26.7 8.9 %collective-permute-start = (f32[8,8,128]{2,1,0:T(8,128)}, f32[8,8,128]{2,1,0:T(8,128)S(1)}, u32[]{:S(2)}, u32[]{:S(2)}) collective-permute-start(f32[8,8,128]{2,1,0:T(8,128)} %combine.1.fields_ref), channel_id=1, source_target_pairs={{0,1},{1,2},{2,3},{3,4},{4,5},{5,6},{6,7},{7,8},{8,9},{9,10},{10,1... | collective-permute-start | bytes 98312 | tf_op jit(solution)/shard_map/ppermute | solution.py:262
  28.7 7.0 %copy-start.1 = (f32[8,8,128]{2,1,0:T(8,128)}, f32[8,8,128]{2,1,0:T(8,128)S(1)}, u32[]{:S(2)}) copy-start(f32[8,8,128]{2,1,0:T(8,128)S(1)} %collective-permute-done.1.after_ref) | copy-start | bytes 98308
  35.7 0.6 copy-start.3
  38.5 5.3 %collective-permute-start.3 = (f32[8,8,128]{2,1,0:T(8,128)}, f32[8,8,128]{2,1,0:T(8,128)S(1)}, u32[]{:S(2)}, u32[]{:S(2)}) collective-permute-start(f32[8,8,128]{2,1,0:T(8,128)} %first.1.own_ref.first_ref), channel_id=1, source_target_pairs={{1,0},{2,1},{3,2},{4,3},{5,4},{6,5},{7,6},{8,7},{9,8},{10,9},{11,1... | collective-permute-start | bytes 98312 | tf_op jit(solution)/shard_map/ppermute | solution.py:262
  40.4 8.8 %collective-permute-start.2 = (f32[8,8,128]{2,1,0:T(8,128)}, f32[8,8,128]{2,1,0:T(8,128)S(1)}, u32[]{:S(2)}, u32[]{:S(2)}) collective-permute-start(f32[8,8,128]{2,1,0:T(8,128)} %first.1.own_ref.first_ref), channel_id=1, source_target_pairs={{0,1},{1,2},{2,3},{3,4},{4,5},{5,6},{6,7},{7,8},{8,9},{9,10},{10,1... | collective-permute-start | bytes 98312 | tf_op jit(solution)/shard_map/ppermute | solution.py:262
  43.8 5.4 %copy-start = (f32[8,8,128]{2,1,0:T(8,128)}, f32[8,8,128]{2,1,0:T(8,128)S(1)}, u32[]{:S(2)}) copy-start(f32[8,8,128]{2,1,0:T(8,128)S(1)} %collective-permute-done.3.after_ref) | copy-start | bytes 98308
  49.2 0.6 copy-start.2

commit v2 on v1

v2 whole, which is shorter than its diff:
```python
import jax
import jax.numpy as jnp
import numpy as np
from jax import lax
from jax.experimental import pallas as pl
from jax.experimental.pallas import tpu as pltpu
from jax.sharding import PartitionSpec as P

SCREEN = 16.0
BLOCKS = 8
SLOTS = 4
SHARE = SLOTS * 8 + 8
BOTH = ("scan", "morton")


def plane_table():
    mass = {-1: 1.0, 0: 4.0, 1: 1.0}
    stiff = {-1: -1.0, 0: 2.0, 1: -1.0}
    side = {0: 1, 7: -1}
    table = np.zeros((256, 128), np.float32)
    for group in range(4):
        for row in range(64):
            b = side.get(row // 8) if group in (1, 3) else 0
            c = side.get(row % 8) if group in (2, 3) else 0
            if b is None or c is None:
                continue
            for col in range(64):
                dj = 8 * b + row // 8 - col // 8
                dk = 8 * c + row % 8 - col % 8
                if abs(dj) <= 1 and abs(dk) <= 1:
                    table[64 * group + row, col] = mass[dj] * mass[dk]
                    table[64 * group + row, 64 + col] = stiff[dj] * mass[dk] + mass[dj] * stiff[dk]
    return table


def split(values):
    high = values.astype(jnp.bfloat16)
    low = (values - high.astype(jnp.float32)).astype(jnp.bfloat16)
    return high, low


def nt(left, right):
    return lax.dot_general(left, right, (((1,), (1,)), ((), ())), preferred_element_type=jnp.float32)


def left_half():
    return lax.broadcasted_iota(jnp.int32, (8, 128), 1) < 64


def splat_kernel(target_ref, spots_ref, norms_ref, weights_ref, out_ref, used_ref):
    node = lax.broadcasted_iota(jnp.int32, (8, 128), 0).astype(jnp.float32)
    first_half = left_half()
    nothing = jnp.zeros((64, 128), jnp.float32)
    for row in range(8):
        used_ref[row] = 0
        out_ref[row * SHARE + SLOTS * 8 : (row + 1) * SHARE, :] = jnp.full((8, 128), -1.0, jnp.float32)
    for q in range(16):
        hats, slopes = [], []
        for dim in range(3):
            diff = spots_ref[dim, q : q + 1, :] - node
            dist = jnp.abs(diff)
            hats.append(jnp.maximum(0.0, 1.0 - dist))
            way = jnp.where(diff > 0.0, -1.0, jnp.where(diff < 0.0, 1.0, 0.0))
            slopes.append(jnp.where(dist < 1.0, way, 0.0))
        weight = weights_ref[q : q + 1, :]
        one = weight * norms_ref[0, q : q + 1, :] * slopes[0]
        two = weight * hats[0]
        three = SCREEN * two * hats[0]
        slope1 = norms_ref[1, q : q + 1, :] * slopes[1]
        slope2 = norms_ref[2, q : q + 1, :] * slopes[2]
        square1 = hats[1] * hats[1]
        square2 = hats[2] * hats[2]
        first = jnp.concatenate([hats[1][j : j + 1] * hats[2] for j in range(8)], axis=0)
        second = jnp.concatenate(
            [slope1[j : j + 1] * hats[2] + hats[1][j : j + 1] * slope2 for j in range(8)], axis=0
        )
        outer = jnp.concatenate([square1[j : j + 1] * square2 for j in range(8)], axis=0)
        right = jnp.concatenate(
            [jnp.concatenate([first, second], axis=1), jnp.concatenate([outer, nothing], axis=1)], axis=0
        )
        left = jnp.concatenate(
            [
                jnp.concatenate([one, two], axis=1),
                jnp.concatenate([three, jnp.zeros((8, 128), jnp.float32)], axis=1),
            ],
            axis=0,
        )
        right_high, right_low = split(right)
        left_high, left_low = split(left)
        main = nt(jnp.concatenate([left_high, left_low], axis=0), right_high)
        total = main[:16] + main[16:] + nt(left_high, right_low)
        target = target_ref[q]
        row = target // (16 * BLOCKS)
        slot = used_ref[row]
        used_ref[row] = slot + 1
        place = pl.multiple_of(row * SHARE + slot * 8, 8)
        out_ref[pl.ds(place, 8), :] = jnp.where(first_half, total[:8], total[8:])
        block = (target % BLOCKS).astype(jnp.float32)
        out_ref[pl.ds(row * SHARE + SLOTS * 8 + slot, 1), :] = jnp.full((1, 128), block, jnp.float32)


def combine_kernel(parts_ref, near_ref, out_ref):
    sums = [jnp.zeros((8, 128), jnp.float32) for _ in range(BLOCKS)]
    for source in range(8):
        for slot in range(SLOTS):
            at = source * SHARE
            part = parts_ref[at + slot * 8 : at + slot * 8 + 8, :]
            name = jnp.broadcast_to(parts_ref[at + SLOTS * 8 + slot : at + SLOTS * 8 + slot + 1, :], (8, 128))
            for block in range(BLOCKS):
                sums[block] = sums[block] + jnp.where(name == float(block), part, 0.0)
    for block in range(BLOCKS):
        out_ref[block] = sums[block]
    out_ref[BLOCKS] = jnp.full((8, 128), -1.0, jnp.float32)
    out_ref[BLOCKS, :, 0:27] = near_ref[...].astype(jnp.float32)


def doubled(tile, first_half):
    return jnp.where(first_half, tile, pltpu.roll(tile, 64, 1))


def couple(index_ref, first_row, blocks, wide_ref, rows_ref, table_ref):
    lane = lax.broadcasted_iota(jnp.int32, (8, 128), 1)
    sublane = lax.broadcasted_iota(jnp.int32, (8, 128), 0)
    first_half = lane < 64
    low_j = lane % 64 < 32
    low_k = lane % 8 < 4
    top = sublane == 0
    bottom = sublane == 7

    def tiles(block, shift):
        def plane(b, c):
            return wide_ref[index_ref[first_row + block, shift + 3 * (b + 1) + c + 1]]

        one = jnp.where(first_half, plane(0, 0), jnp.where(low_j, plane(1, 0), plane(-1, 0)))
        edges = jnp.where(low_k, plane(0, 1), plane(0, -1))
        corners = jnp.where(
            low_j,
            jnp.where(low_k, plane(1, 1), plane(1, -1)),
            jnp.where(low_k, plane(-1, 1), plane(-1, -1)),
        )
        return one, jnp.where(first_half, edges, corners)

    for block in range(blocks):
        before = tiles(block, 0)
        here = tiles(block, 9)
        after = tiles(block, 18)
        ends = [jnp.where(top, late, early) for early, late in zip(before, after)]
        rows = jnp.concatenate(
            [jnp.concatenate([here[half], ends[half]], axis=0) for half in range(2)], axis=1
        )
        high, low = split(rows)
        rows_ref[16 * block : 16 * block + 16, :] = high
        rows_ref[16 * (blocks + block) : 16 * (blocks + block) + 16, :] = low
    both = jnp.dot(rows_ref[0 : 32 * blocks, :], table_ref[...], preferred_element_type=jnp.float32)
    centre = jnp.where(first_half, 2.0 / 36.0, 4.0 / 36.0)
    side = jnp.where(first_half, -1.0 / 36.0, 1.0 / 36.0)
    result = []
    for block in range(blocks):
        at, other = 16 * block, 16 * (blocks + block)
        here = both[at : at + 8] + both[other : other + 8]
        ends = both[at + 8 : at + 16] + both[other + 8 : other + 16]
        before = pltpu.roll(jnp.where(bottom, ends, here), 1, 0)
        after = pltpu.roll(jnp.where(top, ends, here), 7, 0)
        value = centre * here + side * (before + after)
        result.append(value + pltpu.roll(value, 64, 1))
    return result


def total(lefts, rights, first_half):
    terms = [a * b for a, b in zip(lefts, rights)]
    while len(terms) > 1:
        terms = [a + b for a, b in zip(terms[::2], terms[1::2])]
    return jnp.sum(jnp.where(first_half, terms[0], 0.0), axis=(0, 1), keepdims=True)


def image_kernel(
    own_ref,
    one_ref,
    other_ref,
    far_ref,
    rest_ref,
    table_ref,
    first_ref,
    second_ref,
    sums_ref,
    wide_ref,
    next_ref,
    screen_ref,
    names_ref,
    index_ref,
    rows_ref,
    done_ref,
):
    first_half = left_half()
    me = lax.axis_index("scan") * lax.axis_size("morton") + lax.axis_index("morton")
    odd = lax.rem(me, 2)
    late = lax.rem(me, 4) // 2
    base = (me - 2) * BLOCKS
    near = ((own_ref, 2), (one_ref, 3 - 2 * odd), (other_ref, 1 + 2 * odd))
    far = ((far_ref, 4 - 4 * late), (rest_ref, 4 * late))
    for ref, place in near:
        named = ref[BLOCKS].astype(jnp.int32)
        local = named - base
        known = (named >= 0) & (local >= 0) & (local < 5 * BLOCKS)
        names_ref[pl.ds(pl.multiple_of((place - 1) * BLOCKS, 8), 8), :] = jnp.where(known, local, 5 * BLOCKS)
    copy = pltpu.make_async_copy(names_ref, index_ref, done_ref)
    copy.start()
    for ref, place in near + far:
        for block in range(BLOCKS):
            wide_ref[place * BLOCKS + block] = doubled(ref[block], first_half)
    for ref, place in near:
        for block in range(BLOCKS):
            tile = ref[block]
            screen_ref[(place - 1) * BLOCKS + block] = jnp.where(first_half, pltpu.roll(tile, 64, 1), tile)
    nothing = jnp.zeros((8, 128), jnp.float32)
    wide_ref[5 * BLOCKS] = nothing
    next_ref[5 * BLOCKS] = nothing
    copy.wait()
    coupled = couple(index_ref, 0, 3 * BLOCKS, wide_ref, rows_ref, table_ref)
    first = []
    for block in range(3 * BLOCKS):
        image = screen_ref[block] * wide_ref[BLOCKS + block] + coupled[block]
        next_ref[BLOCKS + block] = image
        if BLOCKS <= block < 2 * BLOCKS:
            first_ref[block - BLOCKS] = image
            first.append(image)
    coupled = couple(index_ref, BLOCKS, BLOCKS, next_ref, rows_ref, table_ref)
    second = []
    for block in range(BLOCKS):
        image = screen_ref[BLOCKS + block] * first[block] + coupled[block]
        second_ref[block] = image
        second.append(image)
    start = [wide_ref[2 * BLOCKS + block] for block in range(BLOCKS)]
    lane = lax.broadcasted_iota(jnp.int32, (1, 128), 1)
    packed = jnp.zeros((1, 128), jnp.float32)
    pairs = ((start, start), (start, first), (first, first), (start, second), (first, second))
    for place, (a, b) in enumerate(pairs):
        packed = jnp.where(lane == place, total(a, b, first_half), packed)
    sums_ref[...] = jnp.broadcast_to(packed, (128, 128))


def last_kernel(sums_ref, fields_ref, first_ref, second_ref, solution_ref, residual_ref, left_ref, right_ref):
    first_half = left_half()
    sums = jnp.sum(sums_ref[...], axis=0, keepdims=True)
    lane = lax.broadcasted_iota(jnp.int32, (1, 128), 1)

    def pick(place):
        return jnp.sum(jnp.where(lane == place, sums, 0.0), axis=1, keepdims=True)

    s00, s01, s11, s02, s12 = (pick(place) for place in range(5))
    alpha0 = s00 / s01
    norm1 = s00 - 2.0 * alpha0 * s01 + alpha0 * alpha0 * s11
    beta = norm1 / s00
    grow = 1.0 + beta
    curve = grow * grow * s01 - grow * alpha0 * (s02 + s11) + alpha0 * alpha0 * s12
    alpha1 = norm1 / curve
    for block in range(BLOCKS):
        start = doubled(fields_ref[block], first_half)
        first = first_ref[block]
        left = start - alpha0 * first
        direction = left + beta * start
        image = grow * first - alpha0 * second_ref[block]
        left_ref[block] = alpha0 * start + alpha1 * direction
        right_ref[block] = left - alpha1 * image
    for pair in range(4):
        lanes = slice(128 * pair, 128 * pair + 128)
        solution_ref[:, lanes] = jnp.where(first_half, left_ref[:, 2 * pair, :], left_ref[:, 2 * pair + 1, :])
        residual_ref[:, lanes] = jnp.where(first_half, right_ref[:, 2 * pair, :], right_ref[:, 2 * pair + 1, :])


def vmem(count):
    return [pl.BlockSpec(memory_space=pltpu.VMEM)] * count


def smem(count):
    return [pl.BlockSpec(memory_space=pltpu.SMEM)] * count


def shape(*dims):
    return pltpu.VMEM(dims, jnp.float32)


def resident(values):
    return pltpu.with_memory_space_constraint(values, pltpu.VMEM)


def around(values):
    count = lax.axis_size("scan") * lax.axis_size("morton")
    partners = (
        [i ^ 1 for i in range(count)],
        [(((i + 1) ^ 1) - 1) % count for i in range(count)],
        [i ^ 2 for i in range(count)],
        [(((i + 2) ^ 2) - 2) % count for i in range(count)],
    )
    return [resident(lax.ppermute(values, BOTH, list(enumerate(partner)))) for partner in partners]


def per_device(positions, normals, weights, point_target, neighbours):
    table = resident(jnp.asarray(plane_table(), jnp.bfloat16))
    parts = pl.pallas_call(
        splat_kernel,
        out_shape=shape(8 * SHARE, 128),
        in_specs=smem(1) + vmem(3),
        out_specs=vmem(1)[0],
        scratch_shapes=[pltpu.SMEM((8,), jnp.int32)],
        name="splat",
    )(point_target, positions.transpose(1, 0, 2), normals.transpose(1, 0, 2), weights)
    parts = resident(lax.all_to_all(parts, "scan", 0, 0, tiled=True))
    fields = resident(
        pl.pallas_call(
            combine_kernel,
            out_shape=shape(BLOCKS + 1, 8, 128),
            in_specs=vmem(2),
            out_specs=vmem(1)[0],
            name="combine",
        )(parts, resident(neighbours))
    )
    first, second, sums = pl.pallas_call(
        image_kernel,
        out_shape=(shape(BLOCKS, 8, 128), shape(BLOCKS, 8, 128), shape(128, 128)),
        in_specs=vmem(6),
        out_specs=tuple(vmem(3)),
        scratch_shapes=[
            pltpu.VMEM((5 * BLOCKS + 1, 8, 128), jnp.float32),
            pltpu.VMEM((5 * BLOCKS + 1, 8, 128), jnp.float32),
            pltpu.VMEM((3 * BLOCKS, 8, 128), jnp.float32),
            pltpu.VMEM((3 * BLOCKS, 128), jnp.int32),
            pltpu.SMEM((3 * BLOCKS, 128), jnp.int32),
            pltpu.VMEM((3 * BLOCKS * 32, 256), jnp.bfloat16),
            pltpu.SemaphoreType.DMA,
        ],
        name="images",
    )(fields, *around(fields), table)
    sums = resident(lax.all_to_all(sums, BOTH, 0, 0, tiled=True))
    return pl.pallas_call(
        last_kernel,
        out_shape=(jax.ShapeDtypeStruct((BLOCKS, 512), jnp.float32),) * 2,
        in_specs=vmem(4),
        out_specs=tuple(vmem(2)),
        scratch_shapes=[pltpu.VMEM((BLOCKS, 8, 128), jnp.float32)] * 2,
        name="last",
    )(sums, fields, resident(first), resident(second))


def solution(mesh):
    placed = (
        P(BOTH, None, None),
        P(BOTH, None, None),
        P(BOTH, None),
        P(BOTH),
        P(BOTH, None),
    )
    return jax.shard_map(
        per_device,
        mesh=mesh,
        in_specs=placed,
        out_specs=(P(BOTH, None), P(BOTH, None)),
        check_vma=False,
    )
```

time: 68.5 us -> 46.2 us (0.67)
  waiting for transfers between devices: 12.4 us -> 3.39 us
  Pallas kernels: 10 us -> 4.42 us
  starting transfers between devices: 15.8 us -> 10.6 us
  local copies, waits for them, and re-layouts: 3.21 us -> 0.03 us
  blocking collectives: 25.8 us -> 26.8 us
    ppermute x4, waiting for transfers between devices: 12.4 us -> 3.39 us  [around(): lax.ppermute(values, BOTH, list(enumerate(partner)))]
    ppermute x4, starting transfers between devices: 15.8 us -> 10.6 us  [around(): lax.ppermute(values, BOTH, list(enumerate(partner)))]
    pallas_call x4 -> x3, Pallas kernels: 7.85 us -> 2.92 us  [the longest x1 2.01 us: per_device(): pl.pallas_call(image_kernel, out_shape=(shape(BLOCKS, 8, 128), shape(BLOC...]
    unnamed x12 -> x4, local copies, waits for them, and re-layouts: 3.21 us -> 0.03 us
    all_to_all x2, blocking collectives: 25.8 us -> 26.8 us  [the longest x1 15.5 us: per_device(): sums = resident(lax.all_to_all(sums, BOTH, 0, 0, tiled=True))]
  transfers between devices with their start and end apart: 4 -> 4, of which waited for: 2 -> 3; matrix products, arithmetic and copies ran while one was open for 0% -> 0% of each run, Pallas kernels for 0% -> 0%
where the time goes in v2:
time: 46.2 us; the launch traced here: 45.9 us
  blocking collectives  26.8 us (58%)
  starting transfers between devices  10.6 us (23%)
  Pallas kernels  4.42 us (10%)
  waiting for transfers between devices  3.39 us (7%)
  between operations  0.65 us (1%)
    all_to_all x1, blocking collectives, per_device(): sums = resident(lax.all_to_all(sums, BOTH, 0, 0, tiled=True))  15.5 us
    all_to_all x1, blocking collectives, per_device(): parts = resident(lax.all_to_all(parts, 'scan', 0, 0, tiled=True))  11.4 us
    ppermute x4, starting transfers between devices, around(): lax.ppermute(values, BOTH, list(enumerate(partner)))  10.6 us
    ppermute x4, waiting for transfers between devices, around(): lax.ppermute(values, BOTH, list(enumerate(partner)))  3.39 us
    pallas_call x1, Pallas kernels, per_device(): pl.pallas_call(image_kernel, out_shape=(shape(BLOCKS, 8, 128), shape(BLOC...  2.01 us
    pallas_call x1, Pallas kernels, per_device(): pl.pallas_call(splat_kernel, out_shape=shape(8 * SHARE, 128), in_specs=sm...  1.5 us
  transfers between devices with their start and end apart: 4, of which 3 were waited for; matrix products, arithmetic and copies ran while one was open for 0% of the time, Pallas kernels for 0%

profile of v2, /device:TPU:1, one launch (start us, length us, event | category | flops | bytes accessed | tf_op | source)
XLA Modules:
  0.0 45.9 jit_solution(8593329602808306648)
XLA Ops:
  0.6 1.5 %splat.1 = f32[320,128]{1,0:T(8,128)S(1)} custom-call(s32[16]{0:T(128)} %target_ref.1, f32[3,16,128]{2,1,0:T(8,128)} %bitcast.12, f32[3,16,128]{2,1,0:T(8,128)} %bitcast.13, f32[16,128]{1,0:T(8,128)} %weights_ref.1), custom_call_target="tpu_custom_call" | custom-call | tf_op jit(solution)/shard_map/splat/pallas_call | solution.py:300
  2.1 0.0 copy-start.1
  2.2 11.4 %all_to_all.22 = f32[8,40,128]{2,1,0:T(8,128)S(1)} all-to-all(f32[8,40,128]{2,1,0:T(8,128)S(1)} %bitcast.9), channel_id=1, replica_groups=mesh['scan'=8,'morton'=16] {'scan'}, dimensions={0} | all-to-all | bytes 327680 | tf_op jit(solution)/shard_map/all_to_all | solution.py:308
  13.5 0.0 copy-done.1
  13.5 0.0 copy-start
  13.5 0.1 combine.1.own_ref.fields_ref
  13.6 6.7 %collective-permute-start.3 = (f32[9,8,128]{2,1,0:T(8,128)S(1)}, f32[9,8,128]{2,1,0:T(8,128)S(1)}, u32[]{:S(2)}, u32[]{:S(2)}) collective-permute-start(f32[9,8,128]{2,1,0:T(8,128)S(1)} %combine.1.own_ref.fields_ref), channel_id=1, source_target_pairs={{0,126},{1,127},{2,4},{3,5},{4,2},{5,3},{6,8},{7,9},{8,6},{9,7},{1... | collective-permute-start | bytes 110600 | tf_op jit(solution)/shard_map/ppermute | solution.py:295
  20.3 0.0 collective-permute-start.2
  20.3 4.0 %collective-permute-start.1 = (f32[9,8,128]{2,1,0:T(8,128)S(1)}, f32[9,8,128]{2,1,0:T(8,128)S(1)}, u32[]{:S(2)}, u32[]{:S(2)}) collective-permute-start(f32[9,8,128]{2,1,0:T(8,128)S(1)} %combine.1.own_ref.fields_ref), channel_id=1, source_target_pairs={{0,127},{1,2},{2,1},{3,4},{4,3},{5,6},{6,5},{7,8},{8,7},{9,10},{10... | collective-permute-start | bytes 110600 | tf_op jit(solution)/shard_map/ppermute | solution.py:295
  24.3 0.0 collective-permute-start
  24.3 0.0 collective-permute-done.3.rest_ref
  24.3 0.4 collective-permute-done.2.far_ref
  24.6 2.6 %collective-permute-done.1.other_ref = f32[9,8,128]{2,1,0:T(8,128)S(1)} collective-permute-done((f32[9,8,128]{2,1,0:T(8,128)S(1)}, f32[9,8,128]{2,1,0:T(8,128)S(1)}, u32[]{:S(2)}, u32[]{:S(2)}) %collective-permute-start.1) | collective-permute-done | bytes 36896 | tf_op jit(solution)/shard_map/ppermute | solution.py:295
  27.2 0.4 collective-permute-done.one_ref
  27.7 0.0 copy-done
  27.7 2.0 %images.1 = (f32[8,8,128]{2,1,0:T(8,128)S(1)}, f32[8,8,128]{2,1,0:T(8,128)S(1)}, f32[128,128]{1,0:T(8,128)S(1)}) custom-call(f32[9,8,128]{2,1,0:T(8,128)S(1)} %combine.1.own_ref.fields_ref, f32[9,8,128]{2,1,0:T(8,128)S(1)} %collective-permute-done.one_ref, f32[9,8,128]{2,1,0:T(8,128)S(1)} %collective-permute-done.1.other_ref, ...), custom_call_target="tpu_custom_call" | custom-call | tf_op jit(solution)/shard_map/images/pallas_call | solution.py:318
  29.7 15.5 %all_to_all.23 = f32[128,1,128]{2,1,0:T(1,128)S(1)} all-to-all(f32[128,1,128]{2,1,0:T(1,128)S(1)} %bitcast.11), channel_id=1, replica_groups=mesh['scan'=8,'morton'=16] {'scan','morton'}, dimensions={0} | all-to-all | bytes 131072 | tf_op jit(solution)/shard_map/all_to_all | solution.py:334
  45.2 0.8 %last.1 = (f32[8,512]{1,0:T(8,128)}, f32[8,512]{1,0:T(8,128)}) custom-call(f32[128,128]{1,0:T(8,128)S(1)} %bitcast.10, f32[9,8,128]{2,1,0:T(8,128)S(1)} %combine.1.own_ref.fields_ref, f32[8,8,128]{2,1,0:T(8,128)S(1)} %get-tuple-element.6.first_ref, f32[8,8,128]{2,1,0:T(8,128)S(1)} %get-tuple-element.7.second_ref), custom_call_target="tpu_custom_call" | custom-call | tf_op jit(solution)/shard_map/last/pallas_call | solution.py:335
Async XLA Ops:
  2.1 11.4 %copy-start.1 = (s32[8,27]{1,0:T(8,128)S(1)}, s32[8,27]{1,0:T(8,128)}, u32[]{:S(2)}) copy-start(s32[8,27]{1,0:T(8,128)} %near_ref.1) | copy-start | bytes 2596
  13.5 14.1 %copy-start = (bf16[256,128]{1,0:T(8,128)(2,1)S(1)}, bf16[256,128]{1,0:T(8,128)(2,1)}, u32[]{:S(2)}) copy-start(bf16[256,128]{1,0:T(8,128)(2,1)} %constant.2.clone.table_ref) | copy-start | bytes 196612
  13.6 10.6 %collective-permute-start.3 = (f32[9,8,128]{2,1,0:T(8,128)S(1)}, f32[9,8,128]{2,1,0:T(8,128)S(1)}, u32[]{:S(2)}, u32[]{:S(2)}) collective-permute-start(f32[9,8,128]{2,1,0:T(8,128)S(1)} %combine.1.own_ref.fields_ref), channel_id=1, source_target_pairs={{0,126},{1,127},{2,4},{3,5},{4,2},{5,3},{6,8},{7,9},{8,6},{9,7},{1... | collective-permute-start | bytes 110600 | tf_op jit(solution)/shard_map/ppermute | solution.py:295
  20.3 4.3 %collective-permute-start.2 = (f32[9,8,128]{2,1,0:T(8,128)S(1)}, f32[9,8,128]{2,1,0:T(8,128)S(1)}, u32[]{:S(2)}, u32[]{:S(2)}) collective-permute-start(f32[9,8,128]{2,1,0:T(8,128)S(1)} %combine.1.own_ref.fields_ref), channel_id=1, source_target_pairs={{0,2},{1,3},{2,0},{3,1},{4,6},{5,7},{6,4},{7,5},{8,10},{9,11},{10,... | collective-permute-start | bytes 110600 | tf_op jit(solution)/shard_map/ppermute | solution.py:295
  20.3 6.9 %collective-permute-start.1 = (f32[9,8,128]{2,1,0:T(8,128)S(1)}, f32[9,8,128]{2,1,0:T(8,128)S(1)}, u32[]{:S(2)}, u32[]{:S(2)}) collective-permute-start(f32[9,8,128]{2,1,0:T(8,128)S(1)} %combine.1.own_ref.fields_ref), channel_id=1, source_target_pairs={{0,127},{1,2},{2,1},{3,4},{4,3},{5,6},{6,5},{7,8},{8,7},{9,10},{10... | collective-permute-start | bytes 110600 | tf_op jit(solution)/shard_map/ppermute | solution.py:295
  24.3 3.4 %collective-permute-start = (f32[9,8,128]{2,1,0:T(8,128)S(1)}, f32[9,8,128]{2,1,0:T(8,128)S(1)}, u32[]{:S(2)}, u32[]{:S(2)}) collective-permute-start(f32[9,8,128]{2,1,0:T(8,128)S(1)} %combine.1.own_ref.fields_ref), channel_id=1, source_target_pairs={{0,1},{1,0},{2,3},{3,2},{4,5},{5,4},{6,7},{7,6},{8,9},{9,8},{10,11... | collective-permute-start | bytes 110600 | tf_op jit(solution)/shard_map/ppermute | solution.py:295

commit v3 on v2

--- a/solution.py
+++ b/solution.py
@@ -4,13 +4,15 @@
 from jax import lax
 from jax.experimental import pallas as pl
 from jax.experimental.pallas import tpu as pltpu
+from jax.sharding import Mesh
 from jax.sharding import PartitionSpec as P
 
 SCREEN = 16.0
 BLOCKS = 8
 SLOTS = 4
 SHARE = SLOTS * 8 + 8
-BOTH = ("scan", "morton")
+ALL = ("scan", "pair", "half")
+WINDOW = 6 * BLOCKS
 
 
 def plane_table():
@@ -47,13 +49,18 @@
     return lax.broadcasted_iota(jnp.int32, (8, 128), 1) < 64
 
 
-def splat_kernel(target_ref, spots_ref, norms_ref, weights_ref, out_ref, used_ref):
+def splat_kernel(target_ref, spots_ref, norms_ref, weights_ref, near_ref, out_ref, used_ref, wide_ref):
     node = lax.broadcasted_iota(jnp.int32, (8, 128), 0).astype(jnp.float32)
     first_half = left_half()
     nothing = jnp.zeros((64, 128), jnp.float32)
+    wide_ref[...] = jnp.full((8, 128), -1.0, jnp.float32)
+    wide_ref[:, 0:27] = near_ref[...].astype(jnp.float32)
+    names = jnp.where(first_half, -1.0, pltpu.roll(wide_ref[...], 64, 1))
     for row in range(8):
         used_ref[row] = 0
-        out_ref[row * SHARE + SLOTS * 8 : (row + 1) * SHARE, :] = jnp.full((8, 128), -1.0, jnp.float32)
+        for half in range(2):
+            end = (2 * row + half + 1) * SHARE
+            out_ref[end - 8 : end, :] = names
     for q in range(16):
         hats, slopes = [], []
         for dim in range(3):
@@ -93,32 +100,63 @@
         row = target // (16 * BLOCKS)
         slot = used_ref[row]
         used_ref[row] = slot + 1
-        place = pl.multiple_of(row * SHARE + slot * 8, 8)
-        out_ref[pl.ds(place, 8), :] = jnp.where(first_half, total[:8], total[8:])
+        part = jnp.where(first_half, total[:8], total[8:])
         block = (target % BLOCKS).astype(jnp.float32)
-        out_ref[pl.ds(row * SHARE + SLOTS * 8 + slot, 1), :] = jnp.full((1, 128), block, jnp.float32)
-
-
-def combine_kernel(parts_ref, near_ref, out_ref):
-    sums = [jnp.zeros((8, 128), jnp.float32) for _ in range(BLOCKS)]
-    for source in range(8):
+        for half in range(2):
+            share = (2 * row + half) * SHARE
+            out_ref[pl.ds(pl.multiple_of(share + slot * 8, 8), 8), :] = part
+            out_ref[pl.ds(share + SLOTS * 8 + slot, 1), 0:64] = jnp.full((1, 64), block, jnp.float32)
+
+
+def local_names(table, base):
+    named = table.astype(jnp.int32)
+    local = named - base
+    return jnp.where((named >= 0) & (local >= 0) & (local < WINDOW), local, WINDOW)
+
+
+def window_base():
+    pair = lax.axis_index("scan") * lax.axis_size("pair") + lax.axis_index("pair")
+    return (2 * pair - 2) * BLOCKS
+
+
+def combine_kernel(parts_ref, fields_ref, names_ref, full_ref, edge_ref):
+    first_half = left_half()
+    sums = [[jnp.zeros((8, 128), jnp.float32) for _ in range(BLOCKS)] for _ in range(2)]
+    for source in range(16):
+        at = source * SHARE
+        tile = doubled(parts_ref[at + SLOTS * 8 : at + SLOTS * 8 + 8, :], first_half)
+        into = sums[source % 2]
         for slot in range(SLOTS):
-            at = source * SHARE
             part = parts_ref[at + slot * 8 : at + slot * 8 + 8, :]
-            name = jnp.broadcast_to(parts_ref[at + SLOTS * 8 + slot : at + SLOTS * 8 + slot + 1, :], (8, 128))
+            name = jnp.broadcast_to(tile[slot : slot + 1, :], (8, 128))
             for block in range(BLOCKS):
-                sums[block] = sums[block] + jnp.where(name == float(block), part, 0.0)
+                into[block] = into[block] + jnp.where(name == float(block), part, 0.0)
+    late = lax.axis_index("half") == 1
+    row = 2 * lax.axis_index("scan")
+    tables = []
+    for half in range(2):
+        at = pl.multiple_of((row + half) * SHARE + SLOTS * 8, 8)
+        tables.append(pltpu.roll(parts_ref[pl.ds(at, 8), :], 64, 1))
+        names_ref[half * BLOCKS : half * BLOCKS + BLOCKS, :] = local_names(tables[half], window_base())
+    rest = []
     for block in range(BLOCKS):
-        out_ref[block] = sums[block]
-    out_ref[BLOCKS] = jnp.full((8, 128), -1.0, jnp.float32)
-    out_ref[BLOCKS, :, 0:27] = near_ref[...].astype(jnp.float32)
+        one, two = sums[0][block], sums[1][block]
+        fields_ref[block] = one
+        fields_ref[BLOCKS + block] = two
+        full_ref[block] = jnp.where(late, two, one)
+        rest.append(jnp.where(late, one, two))
+    full_ref[BLOCKS] = jnp.where(late, tables[1], tables[0])
+    for block in range(BLOCKS // 2):
+        tile = jnp.where(first_half, rest[block], pltpu.roll(rest[block + BLOCKS // 2], 64, 1))
+        full_ref[BLOCKS + 1 + block] = tile
+        edge_ref[block] = tile
 
 
 def doubled(tile, first_half):
     return jnp.where(first_half, tile, pltpu.roll(tile, 64, 1))
 
 
-def couple(index_ref, first_row, blocks, wide_ref, rows_ref, table_ref):
+def couple(lookup, blocks, wide_ref, rows_ref, table_ref):
     lane = lax.broadcasted_iota(jnp.int32, (8, 128), 1)
     sublane = lax.broadcasted_iota(jnp.int32, (8, 128), 0)
     first_half = lane < 64
@@ -129,7 +167,7 @@
 
     def tiles(block, shift):
         def plane(b, c):
-            return wide_ref[index_ref[first_row + block, shift + 3 * (b + 1) + c + 1]]
+            return wide_ref[lookup(block, shift + 3 * (b + 1) + c + 1)]
 
         one = jnp.where(first_half, plane(0, 0), jnp.where(low_j, plane(1, 0), plane(-1, 0)))
         edges = jnp.where(low_k, plane(0, 1), plane(0, -1))
@@ -174,11 +212,10 @@
 
 
 def image_kernel(
-    own_ref,
-    one_ref,
-    other_ref,
-    far_ref,
-    rest_ref,
+    pair_ref,
+    fields_ref,
+    full_ref,
+    edge_ref,
     table_ref,
     first_ref,
     second_ref,
@@ -186,57 +223,72 @@
     wide_ref,
     next_ref,
     screen_ref,
+    index_ref,
     names_ref,
-    index_ref,
+    other_ref,
     rows_ref,
+    pair_done_ref,
     done_ref,
 ):
     first_half = left_half()
-    me = lax.axis_index("scan") * lax.axis_size("morton") + lax.axis_index("morton")
-    odd = lax.rem(me, 2)
-    late = lax.rem(me, 4) // 2
-    base = (me - 2) * BLOCKS
-    near = ((own_ref, 2), (one_ref, 3 - 2 * odd), (other_ref, 1 + 2 * odd))
-    far = ((far_ref, 4 - 4 * late), (rest_ref, 4 * late))
-    for ref, place in near:
-        named = ref[BLOCKS].astype(jnp.int32)
-        local = named - base
-        known = (named >= 0) & (local >= 0) & (local < 5 * BLOCKS)
-        names_ref[pl.ds(pl.multiple_of((place - 1) * BLOCKS, 8), 8), :] = jnp.where(known, local, 5 * BLOCKS)
-    copy = pltpu.make_async_copy(names_ref, index_ref, done_ref)
+    half = lax.axis_index("half")
+    pair_copy = pltpu.make_async_copy(pair_ref, index_ref, pair_done_ref)
+    pair_copy.start()
+    names_ref[...] = local_names(full_ref[BLOCKS], window_base())
+    copy = pltpu.make_async_copy(names_ref, other_ref, done_ref)
     copy.start()
-    for ref, place in near + far:
-        for block in range(BLOCKS):
-            wide_ref[place * BLOCKS + block] = doubled(ref[block], first_half)
-    for ref, place in near:
-        for block in range(BLOCKS):
-            tile = ref[block]
-            screen_ref[(place - 1) * BLOCKS + block] = jnp.where(first_half, pltpu.roll(tile, 64, 1), tile)
+    beside = (1 + 3 * half) * BLOCKS
+    packed = 5 * half * BLOCKS
+    across = (4 - 3 * half) * BLOCKS
+    for block in range(2 * BLOCKS):
+        tile = fields_ref[block]
+        turned = pltpu.roll(tile, 64, 1)
+        wide_ref[2 * BLOCKS + block] = jnp.where(first_half, tile, turned)
+        screen_ref[block] = jnp.where(first_half, turned, tile)
+    for block in range(BLOCKS):
+        tile = full_ref[block]
+        turned = pltpu.roll(tile, 64, 1)
+        wide_ref[beside + block] = jnp.where(first_half, tile, turned)
+        screen_ref[2 * BLOCKS + block] = jnp.where(first_half, turned, tile)
+    for block in range(BLOCKS // 2):
+        for tile, place in ((full_ref[BLOCKS + 1 + block], packed), (edge_ref[block], across)):
+            turned = pltpu.roll(tile, 64, 1)
+            wide_ref[place + block] = jnp.where(first_half, tile, turned)
+            wide_ref[place + BLOCKS // 2 + block] = jnp.where(first_half, turned, tile)
     nothing = jnp.zeros((8, 128), jnp.float32)
-    wide_ref[5 * BLOCKS] = nothing
-    next_ref[5 * BLOCKS] = nothing
+    wide_ref[WINDOW] = nothing
+    next_ref[WINDOW] = nothing
+    pair_copy.wait()
     copy.wait()
-    coupled = couple(index_ref, 0, 3 * BLOCKS, wide_ref, rows_ref, table_ref)
-    first = []
+
+    def near(block, offset):
+        if block < 2 * BLOCKS:
+            return index_ref[block, offset]
+        return other_ref[block - 2 * BLOCKS, offset]
+
+    coupled = couple(near, 3 * BLOCKS, wide_ref, rows_ref, table_ref)
     for block in range(3 * BLOCKS):
-        image = screen_ref[block] * wide_ref[BLOCKS + block] + coupled[block]
-        next_ref[BLOCKS + block] = image
-        if BLOCKS <= block < 2 * BLOCKS:
-            first_ref[block - BLOCKS] = image
-            first.append(image)
-    coupled = couple(index_ref, BLOCKS, BLOCKS, next_ref, rows_ref, table_ref)
+        at = 2 * BLOCKS + block if block < 2 * BLOCKS else beside + block - 2 * BLOCKS
+        next_ref[at] = screen_ref[block] * wide_ref[at] + coupled[block]
+    own = (2 + half) * BLOCKS
+    start = [wide_ref[own + block] for block in range(BLOCKS)]
+    first = [next_ref[own + block] for block in range(BLOCKS)]
+
+    def here(block, offset):
+        return index_ref[half * BLOCKS + block, offset]
+
+    coupled = couple(here, BLOCKS, next_ref, rows_ref, table_ref)
     second = []
     for block in range(BLOCKS):
-        image = screen_ref[BLOCKS + block] * first[block] + coupled[block]
-        second_ref[block] = image
-        second.append(image)
-    start = [wide_ref[2 * BLOCKS + block] for block in range(BLOCKS)]
+        second.append(screen_ref[half * BLOCKS + block] * first[block] + coupled[block])
+        first_ref[block] = first[block]
+        second_ref[block] = second[block]
     lane = lax.broadcasted_iota(jnp.int32, (1, 128), 1)
-    packed = jnp.zeros((1, 128), jnp.float32)
+    line = jnp.zeros((1, 128), jnp.float32)
     pairs = ((start, start), (start, first), (first, first), (start, second), (first, second))
     for place, (a, b) in enumerate(pairs):
-        packed = jnp.where(lane == place, total(a, b, first_half), packed)
-    sums_ref[...] = jnp.broadcast_to(packed, (128, 128))
+        line = jnp.where(lane == place, total(a, b, first_half), line)
+    sums_ref[...] = jnp.broadcast_to(line, (128, 128))
 
 
 def last_kernel(sums_ref, fields_ref, first_ref, second_ref, solution_ref, residual_ref, left_ref, right_ref):
@@ -255,7 +307,7 @@
     curve = grow * grow * s01 - grow * alpha0 * (s02 + s11) + alpha0 * alpha0 * s12
     alpha1 = norm1 / curve
     for block in range(BLOCKS):
-        start = doubled(fields_ref[block], first_half)
+        start = doubled(fields_ref[lax.axis_index("half") * BLOCKS + block], first_half)
         first = first_ref[block]
         left = start - alpha0 * first
         direction = left + beta * start
@@ -284,54 +336,56 @@
     return pltpu.with_memory_space_constraint(values, pltpu.VMEM)
 
 
-def around(values):
-    count = lax.axis_size("scan") * lax.axis_size("morton")
-    partners = (
-        [i ^ 1 for i in range(count)],
-        [(((i + 1) ^ 1) - 1) % count for i in range(count)],
-        [i ^ 2 for i in range(count)],
-        [(((i + 2) ^ 2) - 2) % count for i in range(count)],
-    )
-    return [resident(lax.ppermute(values, BOTH, list(enumerate(partner)))) for partner in partners]
+def exchange(values, partners):
+    return resident(lax.ppermute(values, ALL, list(enumerate(partners))))
 
 
 def per_device(positions, normals, weights, point_target, neighbours):
     table = resident(jnp.asarray(plane_table(), jnp.bfloat16))
     parts = pl.pallas_call(
         splat_kernel,
-        out_shape=shape(8 * SHARE, 128),
-        in_specs=smem(1) + vmem(3),
+        out_shape=shape(16 * SHARE, 128),
+        in_specs=smem(1) + vmem(4),
         out_specs=vmem(1)[0],
-        scratch_shapes=[pltpu.SMEM((8,), jnp.int32)],
+        scratch_shapes=[pltpu.SMEM((8,), jnp.int32), pltpu.VMEM((8, 128), jnp.float32)],
         name="splat",
-    )(point_target, positions.transpose(1, 0, 2), normals.transpose(1, 0, 2), weights)
-    parts = resident(lax.all_to_all(parts, "scan", 0, 0, tiled=True))
-    fields = resident(
-        pl.pallas_call(
-            combine_kernel,
-            out_shape=shape(BLOCKS + 1, 8, 128),
-            in_specs=vmem(2),
-            out_specs=vmem(1)[0],
-            name="combine",
-        )(parts, resident(neighbours))
-    )
+    )(point_target, positions.transpose(1, 0, 2), normals.transpose(1, 0, 2), weights, neighbours)
+    parts = resident(lax.all_to_all(parts, ("scan", "half"), 0, 0, tiled=True))
+    fields, names, full, edge = pl.pallas_call(
+        combine_kernel,
+        out_shape=(
+            shape(2 * BLOCKS, 8, 128),
+            pltpu.VMEM((2 * BLOCKS, 128), jnp.int32),
+            shape(BLOCKS + 1 + BLOCKS // 2, 8, 128),
+            shape(BLOCKS // 2, 8, 128),
+        ),
+        in_specs=vmem(1),
+        out_specs=tuple(vmem(4)),
+        name="combine",
+    )(parts)
+    fields = resident(fields)
+    count = lax.axis_size("scan") * lax.axis_size("pair") * 2
+    full = exchange(full, [(i - 1 + 2 * (i % 2)) % count for i in range(count)])
+    edge = exchange(edge, [(i + 3 - 6 * (i % 2)) % count for i in range(count)])
     first, second, sums = pl.pallas_call(
         image_kernel,
         out_shape=(shape(BLOCKS, 8, 128), shape(BLOCKS, 8, 128), shape(128, 128)),
-        in_specs=vmem(6),
+        in_specs=vmem(5),
         out_specs=tuple(vmem(3)),
         scratch_shapes=[
-            pltpu.VMEM((5 * BLOCKS + 1, 8, 128), jnp.float32),
-            pltpu.VMEM((5 * BLOCKS + 1, 8, 128), jnp.float32),
+            pltpu.VMEM((WINDOW + 1, 8, 128), jnp.float32),
+            pltpu.VMEM((WINDOW + 1, 8, 128), jnp.float32),
             pltpu.VMEM((3 * BLOCKS, 8, 128), jnp.float32),
-            pltpu.VMEM((3 * BLOCKS, 128), jnp.int32),
-            pltpu.SMEM((3 * BLOCKS, 128), jnp.int32),
+            pltpu.SMEM((2 * BLOCKS, 128), jnp.int32),
+            pltpu.VMEM((BLOCKS, 128), jnp.int32),
+            pltpu.SMEM((BLOCKS, 128), jnp.int32),
             pltpu.VMEM((3 * BLOCKS * 32, 256), jnp.bfloat16),
+            pltpu.SemaphoreType.DMA,
             pltpu.SemaphoreType.DMA,
         ],
         name="images",
-    )(fields, *around(fields), table)
-    sums = resident(lax.all_to_all(sums, BOTH, 0, 0, tiled=True))
+    )(resident(names), fields, full, edge, table)
+    sums = resident(lax.all_to_all(sums, ALL, 0, 0, tiled=True))
     return pl.pallas_call(
         last_kernel,
         out_shape=(jax.ShapeDtypeStruct((BLOCKS, 512), jnp.float32),) * 2,
@@ -343,17 +397,13 @@
 
 
 def solution(mesh):
-    placed = (
-        P(BOTH, None, None),
-        P(BOTH, None, None),
-        P(BOTH, None),
-        P(BOTH),
-        P(BOTH, None),
-    )
+    scan, morton = mesh.devices.shape
+    paired = Mesh(mesh.devices.reshape(scan, morton // 2, 2), ALL)
+    placed = (P(ALL, None, None), P(ALL, None, None), P(ALL, None), P(ALL), P(ALL, None))
     return jax.shard_map(
         per_device,
-        mesh=mesh,
+        mesh=paired,
         in_specs=placed,
-        out_specs=(P(BOTH, None), P(BOTH, None)),
+        out_specs=(P(ALL, None), P(ALL, None)),
         check_vma=False,
     )

time: 46.2 us -> 45.7 us (0.989)
  starting transfers between devices: 10.6 us -> 4.95 us
  blocking collectives: 26.8 us -> 31.1 us
  waiting for transfers between devices: 3.39 us -> 4.11 us
    ppermute x4 -> x2, starting transfers between devices: 10.6 us -> 4.95 us  [exchange(): return resident(lax.ppermute(values, ALL, list(enumerate(partners))))]
    all_to_all x2, blocking collectives: 26.8 us -> 31.1 us  [the longest x1 15.7 us: per_device(): parts = resident(lax.all_to_all(parts, ('scan', 'half'), 0, 0, tiled=True))]
    ppermute x4 -> x2, waiting for transfers between devices: 3.39 us -> 4.11 us  [exchange(): return resident(lax.ppermute(values, ALL, list(enumerate(partners))))]
  transfers between devices with their start and end apart: 4 -> 2, of which waited for: 3 -> 1; matrix products, arithmetic and copies ran while one was open for 0% -> 0% of each run, Pallas kernels for 0% -> 0%
where the time goes in v3:
time: 45.7 us; the launch traced here: 45.5 us
  blocking collectives  31.1 us (68%)
  starting transfers between devices  4.95 us (11%)
  Pallas kernels  4.66 us (10%)
  waiting for transfers between devices  4.11 us (9%)
  between operations  0.66 us (1%)
    all_to_all x1, blocking collectives, per_device(): parts = resident(lax.all_to_all(parts, ('scan', 'half'), 0, 0, tiled=True))  15.7 us
    all_to_all x1, blocking collectives, per_device(): sums = resident(lax.all_to_all(sums, ALL, 0, 0, tiled=True))  15.5 us
    ppermute x2, starting transfers between devices, exchange(): return resident(lax.ppermute(values, ALL, list(enumerate(partners))))  4.95 us
    ppermute x2, waiting for transfers between devices, exchange(): return resident(lax.ppermute(values, ALL, list(enumerate(partners))))  4.11 us
    pallas_call x1, Pallas kernels, per_device(): pl.pallas_call(image_kernel, out_shape=(shape(BLOCKS, 8, 128), shape(BLOC...  2.06 us
    pallas_call x1, Pallas kernels, per_device(): pl.pallas_call(splat_kernel, out_shape=shape(16 * SHARE, 128), in_specs=s...  1.5 us
  transfers between devices with their start and end apart: 2, of which 1 were waited for; matrix products, arithmetic and copies ran while one was open for 0% of the time, Pallas kernels for 0%

profile of v3, /device:TPU:1, one launch (start us, length us, event | category | flops | bytes accessed | tf_op | source)
XLA Modules:
  0.0 45.5 jit_solution(11230043669641430849)
XLA Ops:
  0.6 1.5 %splat.1 = f32[640,128]{1,0:T(8,128)S(1)} custom-call(s32[16]{0:T(128)} %target_ref.1, f32[3,16,128]{2,1,0:T(8,128)} %bitcast.12, f32[3,16,128]{2,1,0:T(8,128)} %bitcast.13, f32[16,128]{1,0:T(8,128)} %weights_ref.1, s32[8,27]{1,0:T(8,128)} %near_ref.1), custom_call_target="tpu_custom_call" | custom-call | tf_op jit(solution)/shard_map/splat/pallas_call | solution.py:345
  2.2 15.7 %all_to_all.22 = f32[16,40,128]{2,1,0:T(8,128)S(1)} all-to-all(f32[16,40,128]{2,1,0:T(8,128)S(1)} %bitcast.9), channel_id=1, replica_groups=mesh['scan'=8,'pair'=8,'half'=2] {'scan','half'}, dimensions={0} | all-to-all | bytes 655360 | tf_op jit(solution)/shard_map/all_to_all | solution.py:353
  17.8 0.0 copy-start
  17.8 0.3 combine.1
  18.1 5.0 %collective-permute-start = (f32[13,8,128]{2,1,0:T(8,128)S(1)}, f32[13,8,128]{2,1,0:T(8,128)S(1)}, u32[]{:S(2)}, u32[]{:S(2)}) collective-permute-start(f32[13,8,128]{2,1,0:T(8,128)S(1)} %get-tuple-element.11), channel_id=1, source_target_pairs={{0,127},{1,2},{2,1},{3,4},{4,3},{5,6},{6,5},{7,8},{8,7},{9,10},{10... | collective-permute-start | bytes 159752 | tf_op jit(solution)/shard_map/ppermute | solution.py:340
  23.1 0.0 collective-permute-start.1
  23.1 4.1 %collective-permute-done.1.edge_ref = f32[4,8,128]{2,1,0:T(8,128)S(1)} collective-permute-done((f32[4,8,128]{2,1,0:T(8,128)S(1)}, f32[4,8,128]{2,1,0:T(8,128)S(1)}, u32[]{:S(2)}, u32[]{:S(2)}) %collective-permute-start.1) | collective-permute-done | bytes 16416 | tf_op jit(solution)/shard_map/ppermute | solution.py:340
  27.2 0.0 collective-permute-done.full_ref
  27.2 0.0 copy-done
  27.2 2.1 %images.1 = (f32[8,8,128]{2,1,0:T(8,128)S(1)}, f32[8,8,128]{2,1,0:T(8,128)S(1)}, f32[128,128]{1,0:T(8,128)S(1)}) custom-call(s32[16,128]{1,0:T(8,128)S(1)} %get-tuple-element.9.pair_ref, f32[16,8,128]{2,1,0:T(8,128)S(1)} %get-tuple-element.10.fields_ref, f32[13,8,128]{2,1,0:T(8,128)S(1)} %collective-permute-done.full_ref, ...), custom_call_target="tpu_custom_call" | custom-call | tf_op jit(solution)/shard_map/images/pallas_call | solution.py:370
  29.3 15.5 %all_to_all.23 = f32[128,1,128]{2,1,0:T(1,128)S(1)} all-to-all(f32[128,1,128]{2,1,0:T(1,128)S(1)} %bitcast.11), channel_id=1, replica_groups=mesh['scan'=8,'pair'=8,'half'=2] {'scan','pair','half'}, dimensions={0} | all-to-all | bytes 131072 | tf_op jit(solution)/shard_map/all_to_all | solution.py:388
  44.7 0.8 %last.1 = (f32[8,512]{1,0:T(8,128)}, f32[8,512]{1,0:T(8,128)}) custom-call(f32[128,128]{1,0:T(8,128)S(1)} %bitcast.10, f32[16,8,128]{2,1,0:T(8,128)S(1)} %get-tuple-element.10.fields_ref, f32[8,8,128]{2,1,0:T(8,128)S(1)} %get-tuple-element.14.first_ref, f32[8,8,128]{2,1,0:T(8,128)S(1)} %get-tuple-element.15.second_ref), custom_call_target="tpu_custom_call" | custom-call | tf_op jit(solution)/shard_map/last/pallas_call | solution.py:389
Async XLA Ops:
  17.8 9.4 %copy-start = (bf16[256,128]{1,0:T(8,128)(2,1)S(1)}, bf16[256,128]{1,0:T(8,128)(2,1)}, u32[]{:S(2)}) copy-start(bf16[256,128]{1,0:T(8,128)(2,1)} %constant.2.clone.table_ref) | copy-start | bytes 196612
  18.1 9.1 %collective-permute-start = (f32[13,8,128]{2,1,0:T(8,128)S(1)}, f32[13,8,128]{2,1,0:T(8,128)S(1)}, u32[]{:S(2)}, u32[]{:S(2)}) collective-permute-start(f32[13,8,128]{2,1,0:T(8,128)S(1)} %get-tuple-element.11), channel_id=1, source_target_pairs={{0,127},{1,2},{2,1},{3,4},{4,3},{5,6},{6,5},{7,8},{8,7},{9,10},{10... | collective-permute-start | bytes 159752 | tf_op jit(solution)/shard_map/ppermute | solution.py:340
  23.1 4.1 %collective-permute-start.1 = (f32[4,8,128]{2,1,0:T(8,128)S(1)}, f32[4,8,128]{2,1,0:T(8,128)S(1)}, u32[]{:S(2)}, u32[]{:S(2)}) collective-permute-start(f32[4,8,128]{2,1,0:T(8,128)S(1)} %get-tuple-element.12), channel_id=1, source_target_pairs={{0,3},{1,126},{2,5},{3,0},{4,7},{5,2},{6,9},{7,4},{8,11},{9,6},{10... | collective-permute-start | bytes 49160 | tf_op jit(solution)/shard_map/ppermute | solution.py:340

commit v4 on v2

--- a/solution.py
+++ b/solution.py
@@ -4,13 +4,15 @@
 from jax import lax
 from jax.experimental import pallas as pl
 from jax.experimental.pallas import tpu as pltpu
+from jax.sharding import Mesh
 from jax.sharding import PartitionSpec as P
 
 SCREEN = 16.0
 BLOCKS = 8
 SLOTS = 4
 SHARE = SLOTS * 8 + 8
-BOTH = ("scan", "morton")
+ALL = ("scan", "quad", "place")
+WINDOW = 8 * BLOCKS
 
 
 def plane_table():
@@ -99,6 +101,17 @@
         out_ref[pl.ds(row * SHARE + SLOTS * 8 + slot, 1), :] = jnp.full((1, 128), block, jnp.float32)
 
 
+def local_names(table, base):
+    named = table.astype(jnp.int32)
+    local = named - base
+    return jnp.where((named >= 0) & (local >= 0) & (local < WINDOW), 8 * local, 8 * WINDOW)
+
+
+def window_base():
+    quad = lax.axis_index("scan") * lax.axis_size("quad") + lax.axis_index("quad")
+    return (4 * quad - 2) * BLOCKS
+
+
 def combine_kernel(parts_ref, near_ref, out_ref):
     sums = [jnp.zeros((8, 128), jnp.float32) for _ in range(BLOCKS)]
     for source in range(8):
@@ -114,11 +127,26 @@
     out_ref[BLOCKS, :, 0:27] = near_ref[...].astype(jnp.float32)
 
 
+def pack_kernel(own_ref, beside_ref, out_ref):
+    for block in range(BLOCKS):
+        out_ref[block] = own_ref[block]
+        out_ref[BLOCKS + block] = beside_ref[block]
+    out_ref[2 * BLOCKS] = jnp.where(left_half(), own_ref[BLOCKS], pltpu.roll(beside_ref[BLOCKS], 64, 1))
+
+
 def doubled(tile, first_half):
     return jnp.where(first_half, tile, pltpu.roll(tile, 64, 1))
 
 
-def couple(index_ref, first_row, blocks, wide_ref, rows_ref, table_ref):
+def rows_at(first):
+    return pl.ds(pl.multiple_of(first, 8), 8)
+
+
+def tile_at(block):
+    return rows_at(8 * block)
+
+
+def couple(lookup, blocks, wide_ref, rows_ref, table_ref):
     lane = lax.broadcasted_iota(jnp.int32, (8, 128), 1)
     sublane = lax.broadcasted_iota(jnp.int32, (8, 128), 0)
     first_half = lane < 64
@@ -129,7 +157,7 @@
 
     def tiles(block, shift):
         def plane(b, c):
-            return wide_ref[index_ref[first_row + block, shift + 3 * (b + 1) + c + 1]]
+            return wide_ref[rows_at(lookup(block, shift + 3 * (b + 1) + c + 1)), :]
 
         one = jnp.where(first_half, plane(0, 0), jnp.where(low_j, plane(1, 0), plane(-1, 0)))
         edges = jnp.where(low_k, plane(0, 1), plane(0, -1))
@@ -176,9 +204,8 @@
 def image_kernel(
     own_ref,
     one_ref,
-    other_ref,
-    far_ref,
-    rest_ref,
+    two_ref,
+    three_ref,
     table_ref,
     first_ref,
     second_ref,
@@ -192,51 +219,56 @@
     done_ref,
 ):
     first_half = left_half()
-    me = lax.axis_index("scan") * lax.axis_size("morton") + lax.axis_index("morton")
-    odd = lax.rem(me, 2)
-    late = lax.rem(me, 4) // 2
-    base = (me - 2) * BLOCKS
-    near = ((own_ref, 2), (one_ref, 3 - 2 * odd), (other_ref, 1 + 2 * odd))
-    far = ((far_ref, 4 - 4 * late), (rest_ref, 4 * late))
-    for ref, place in near:
-        named = ref[BLOCKS].astype(jnp.int32)
-        local = named - base
-        known = (named >= 0) & (local >= 0) & (local < 5 * BLOCKS)
-        names_ref[pl.ds(pl.multiple_of((place - 1) * BLOCKS, 8), 8), :] = jnp.where(known, local, 5 * BLOCKS)
-    copy = pltpu.make_async_copy(names_ref, index_ref, done_ref)
+    place = lax.axis_index("place")
+    parts = []
+    for step, ref in enumerate((own_ref, one_ref, two_ref, three_ref)):
+        member = lax.bitwise_xor(place, step)
+        parts.append((ref, (2 + member) * BLOCKS, lax.rem(member + 6, 8) * BLOCKS))
+    for ref, inner, outer in parts:
+        tile = ref[2 * BLOCKS]
+        names_ref[pl.ds(pl.multiple_of(inner, 8), 8), :] = local_names(tile, window_base())
+        names_ref[pl.ds(pl.multiple_of(outer, 8), 8), :] = local_names(pltpu.roll(tile, 64, 1), window_base())
+    copy = pltpu.make_async_copy(names_ref.at[pl.ds(BLOCKS, 6 * BLOCKS)], index_ref, done_ref)
     copy.start()
-    for ref, place in near + far:
-        for block in range(BLOCKS):
-            wide_ref[place * BLOCKS + block] = doubled(ref[block], first_half)
-    for ref, place in near:
-        for block in range(BLOCKS):
+    for ref, inner, outer in parts:
+        for block in range(2 * BLOCKS):
+            at = inner + block if block < BLOCKS else outer + block - BLOCKS
             tile = ref[block]
-            screen_ref[(place - 1) * BLOCKS + block] = jnp.where(first_half, pltpu.roll(tile, 64, 1), tile)
+            turned = pltpu.roll(tile, 64, 1)
+            wide_ref[tile_at(at), :] = jnp.where(first_half, tile, turned)
+            screen_ref[tile_at(at), :] = jnp.where(first_half, turned, tile)
     nothing = jnp.zeros((8, 128), jnp.float32)
-    wide_ref[5 * BLOCKS] = nothing
-    next_ref[5 * BLOCKS] = nothing
+    wide_ref[tile_at(WINDOW), :] = nothing
+    next_ref[tile_at(WINDOW), :] = nothing
     copy.wait()
-    coupled = couple(index_ref, 0, 3 * BLOCKS, wide_ref, rows_ref, table_ref)
-    first = []
-    for block in range(3 * BLOCKS):
-        image = screen_ref[block] * wide_ref[BLOCKS + block] + coupled[block]
-        next_ref[BLOCKS + block] = image
-        if BLOCKS <= block < 2 * BLOCKS:
-            first_ref[block - BLOCKS] = image
-            first.append(image)
-    coupled = couple(index_ref, BLOCKS, BLOCKS, next_ref, rows_ref, table_ref)
+
+    def near(block, offset):
+        return index_ref[block, offset]
+
+    def inside(block, offset):
+        return index_ref[BLOCKS + block, offset]
+
+    coupled = couple(near, 6 * BLOCKS, wide_ref, rows_ref, table_ref)
+    for block in range(6 * BLOCKS):
+        at = BLOCKS + block
+        next_ref[tile_at(at), :] = screen_ref[tile_at(at), :] * wide_ref[tile_at(at), :] + coupled[block]
+    start = [wide_ref[tile_at(2 * BLOCKS + block), :] for block in range(4 * BLOCKS)]
+    first = [next_ref[tile_at(2 * BLOCKS + block), :] for block in range(4 * BLOCKS)]
+    coupled = couple(inside, 4 * BLOCKS, next_ref, rows_ref, table_ref)
     second = []
+    for block in range(4 * BLOCKS):
+        image = screen_ref[tile_at(2 * BLOCKS + block), :] * first[block] + coupled[block]
+        second.append(image)
+        wide_ref[tile_at(block), :] = image
     for block in range(BLOCKS):
-        image = screen_ref[BLOCKS + block] * first[block] + coupled[block]
-        second_ref[block] = image
-        second.append(image)
-    start = [wide_ref[2 * BLOCKS + block] for block in range(BLOCKS)]
+        first_ref[block] = next_ref[tile_at((2 + place) * BLOCKS + block), :]
+        second_ref[block] = wide_ref[tile_at(place * BLOCKS + block), :]
     lane = lax.broadcasted_iota(jnp.int32, (1, 128), 1)
-    packed = jnp.zeros((1, 128), jnp.float32)
+    line = jnp.zeros((1, 128), jnp.float32)
     pairs = ((start, start), (start, first), (first, first), (start, second), (first, second))
-    for place, (a, b) in enumerate(pairs):
-        packed = jnp.where(lane == place, total(a, b, first_half), packed)
-    sums_ref[...] = jnp.broadcast_to(packed, (128, 128))
+    for slot, (a, b) in enumerate(pairs):
+        line = jnp.where(lane == slot, total(a, b, first_half), line)
+    sums_ref[...] = jnp.broadcast_to(line, (32, 128))
 
 
 def last_kernel(sums_ref, fields_ref, first_ref, second_ref, solution_ref, residual_ref, left_ref, right_ref):
@@ -282,17 +314,6 @@
 
 def resident(values):
     return pltpu.with_memory_space_constraint(values, pltpu.VMEM)
-
-
-def around(values):
-    count = lax.axis_size("scan") * lax.axis_size("morton")
-    partners = (
-        [i ^ 1 for i in range(count)],
-        [(((i + 1) ^ 1) - 1) % count for i in range(count)],
-        [i ^ 2 for i in range(count)],
-        [(((i + 2) ^ 2) - 2) % count for i in range(count)],
-    )
-    return [resident(lax.ppermute(values, BOTH, list(enumerate(partner)))) for partner in partners]
 
 
 def per_device(positions, normals, weights, point_target, neighbours):
@@ -315,23 +336,35 @@
             name="combine",
         )(parts, resident(neighbours))
     )
+    count = lax.axis_size("scan") * lax.axis_size("quad") * 4
+    beside = resident(lax.ppermute(fields, ALL, [(i, (i - 4 if i % 4 < 2 else i + 4) % count) for i in range(count)]))
+    packed = resident(
+        pl.pallas_call(
+            pack_kernel,
+            out_shape=shape(2 * BLOCKS + 1, 8, 128),
+            in_specs=vmem(2),
+            out_specs=vmem(1)[0],
+            name="pack",
+        )(fields, beside)
+    )
+    others = [resident(lax.ppermute(packed, "place", [(i, i ^ step) for i in range(4)])) for step in (1, 2, 3)]
     first, second, sums = pl.pallas_call(
         image_kernel,
-        out_shape=(shape(BLOCKS, 8, 128), shape(BLOCKS, 8, 128), shape(128, 128)),
-        in_specs=vmem(6),
+        out_shape=(shape(BLOCKS, 8, 128), shape(BLOCKS, 8, 128), shape(32, 128)),
+        in_specs=vmem(5),
         out_specs=tuple(vmem(3)),
         scratch_shapes=[
-            pltpu.VMEM((5 * BLOCKS + 1, 8, 128), jnp.float32),
-            pltpu.VMEM((5 * BLOCKS + 1, 8, 128), jnp.float32),
-            pltpu.VMEM((3 * BLOCKS, 8, 128), jnp.float32),
-            pltpu.VMEM((3 * BLOCKS, 128), jnp.int32),
-            pltpu.SMEM((3 * BLOCKS, 128), jnp.int32),
-            pltpu.VMEM((3 * BLOCKS * 32, 256), jnp.bfloat16),
+            pltpu.VMEM((8 * WINDOW + 8, 128), jnp.float32),
+            pltpu.VMEM((8 * WINDOW + 8, 128), jnp.float32),
+            pltpu.VMEM((8 * WINDOW, 128), jnp.float32),
+            pltpu.VMEM((WINDOW, 128), jnp.int32),
+            pltpu.SMEM((6 * BLOCKS, 128), jnp.int32),
+            pltpu.VMEM((6 * BLOCKS * 32, 256), jnp.bfloat16),
             pltpu.SemaphoreType.DMA,
         ],
         name="images",
-    )(fields, *around(fields), table)
-    sums = resident(lax.all_to_all(sums, BOTH, 0, 0, tiled=True))
+    )(packed, *others, table)
+    sums = resident(lax.all_to_all(sums, ("scan", "quad"), 0, 0, tiled=True))
     return pl.pallas_call(
         last_kernel,
         out_shape=(jax.ShapeDtypeStruct((BLOCKS, 512), jnp.float32),) * 2,
@@ -343,17 +376,13 @@
 
 
 def solution(mesh):
-    placed = (
-        P(BOTH, None, None),
-        P(BOTH, None, None),
-        P(BOTH, None),
-        P(BOTH),
-        P(BOTH, None),
-    )
+    scan, morton = mesh.devices.shape
+    grouped = Mesh(mesh.devices.reshape(scan, morton // 4, 4), ALL)
+    placed = (P(ALL, None, None), P(ALL, None, None), P(ALL, None), P(ALL), P(ALL, None))
     return jax.shard_map(
         per_device,
-        mesh=mesh,
+        mesh=grouped,
         in_specs=placed,
-        out_specs=(P(BOTH, None), P(BOTH, None)),
+        out_specs=(P(ALL, None), P(ALL, None)),
         check_vma=False,
     )

time: 46.2 us -> 45 us (0.974)
  blocking collectives: 26.8 us -> 24.7 us
  starting transfers between devices: 10.6 us -> 8.67 us
  waiting for transfers between devices: 3.39 us -> 5.16 us
  Pallas kernels: 4.42 us -> 5.44 us
    all_to_all x1, blocking collectives: 15.5 us -> 13.4 us  [per_device(): sums = resident(lax.all_to_all(sums, ('scan', 'quad'), 0, 0, tiled=True))]
    ppermute x4, starting transfers between devices: 10.6 us -> 8.67 us  [the longest x3 5.32 us: per_device(): lax.ppermute(packed, 'place', [(i, i ^ step) for i in range(4)])]
    ppermute x4, waiting for transfers between devices: 3.39 us -> 5.16 us  [the longest x3 4.1 us: per_device(): lax.ppermute(packed, 'place', [(i, i ^ step) for i in range(4)])]
    pallas_call x1, Pallas kernels: 2.01 us -> 2.98 us  [per_device(): pl.pallas_call(image_kernel, out_shape=(shape(BLOCKS, 8, 128), shape(BLOC...]
where the time goes in v4:
time: 45 us; the launch traced here: 44.7 us
  blocking collectives  24.7 us (55%)
  starting transfers between devices  8.67 us (19%)
  Pallas kernels  5.44 us (12%)
  waiting for transfers between devices  5.16 us (11%)
  between operations  0.66 us (1%)
    all_to_all x1, blocking collectives, per_device(): sums = resident(lax.all_to_all(sums, ('scan', 'quad'), 0, 0, tiled=True))  13.4 us
    all_to_all x1, blocking collectives, per_device(): parts = resident(lax.all_to_all(parts, 'scan', 0, 0, tiled=True))  11.4 us
    ppermute x3, starting transfers between devices, per_device(): lax.ppermute(packed, 'place', [(i, i ^ step) for i in range(4)])  5.32 us
    ppermute x3, waiting for transfers between devices, per_device(): lax.ppermute(packed, 'place', [(i, i ^ step) for i in range(4)])  4.1 us
    ppermute x1, starting transfers between devices, per_device(): lax.ppermute(fields, ALL, [(i, (i - 4 if i % 4 < 2 else i + 4) % count) f...  3.35 us
    pallas_call x1, Pallas kernels, per_device(): pl.pallas_call(image_kernel, out_shape=(shape(BLOCKS, 8, 128), shape(BLOC...  2.98 us
    pallas_call x1, Pallas kernels, per_device(): pl.pallas_call(splat_kernel, out_shape=shape(8 * SHARE, 128), in_specs=sm...  1.5 us
    ppermute x1, waiting for transfers between devices, per_device(): lax.ppermute(fields, ALL, [(i, (i - 4 if i % 4 < 2 else i + 4) % count) f...  1.06 us
  transfers between devices with their start and end apart: 4, of which 3 were waited for; matrix products, arithmetic and copies ran while one was open for 0% of the time, Pallas kernels for 0%

profile of v4, /device:TPU:1, one launch (start us, length us, event | category | flops | bytes accessed | tf_op | source)
XLA Modules:
  0.0 44.7 jit_solution(3764158646668455953)
XLA Ops:
  0.6 1.5 %splat.1 = f32[320,128]{1,0:T(8,128)S(1)} custom-call(s32[16]{0:T(128)} %target_ref.1, f32[3,16,128]{2,1,0:T(8,128)} %bitcast.12, f32[3,16,128]{2,1,0:T(8,128)} %bitcast.13, f32[16,128]{1,0:T(8,128)} %weights_ref.1), custom_call_target="tpu_custom_call" | custom-call | tf_op jit(solution)/shard_map/splat/pallas_call | solution.py:321
  2.1 0.0 copy-start.1
  2.2 11.4 %all_to_all.22 = f32[8,40,128]{2,1,0:T(8,128)S(1)} all-to-all(f32[8,40,128]{2,1,0:T(8,128)S(1)} %bitcast.9), channel_id=1, replica_groups=mesh['scan'=8,'quad'=4,'place'=4] {'scan'}, dimensions={0} | all-to-all | bytes 327680 | tf_op jit(solution)/shard_map/all_to_all | solution.py:329
  13.5 0.0 copy-done.1
  13.5 0.1 combine.1.own_ref.fields_ref
  13.6 0.0 copy-start
  13.6 3.3 %collective-permute-start = (f32[9,8,128]{2,1,0:T(8,128)S(1)}, f32[9,8,128]{2,1,0:T(8,128)S(1)}, u32[]{:S(2)}, u32[]{:S(2)}) collective-permute-start(f32[9,8,128]{2,1,0:T(8,128)S(1)} %combine.1.own_ref.fields_ref), channel_id=1, source_target_pairs={{0,124},{1,125},{2,6},{3,7},{4,0},{5,1},{6,10},{7,11},{8,4},{9,5},... | collective-permute-start | bytes 110600 | tf_op jit(solution)/shard_map/ppermute | solution.py:340
  17.0 1.1 %collective-permute-done.beside_ref = f32[9,8,128]{2,1,0:T(8,128)S(1)} collective-permute-done((f32[9,8,128]{2,1,0:T(8,128)S(1)}, f32[9,8,128]{2,1,0:T(8,128)S(1)}, u32[]{:S(2)}, u32[]{:S(2)}) %collective-permute-start) | collective-permute-done | bytes 36896 | tf_op jit(solution)/shard_map/ppermute | solution.py:340
  18.1 0.1 pack.1.own_ref
  18.1 4.7 %collective-permute-start.3 = (f32[17,8,128]{2,1,0:T(8,128)S(1)}, f32[17,8,128]{2,1,0:T(8,128)S(1)}, u32[]{:S(2)}, u32[]{:S(2)}) collective-permute-start(f32[17,8,128]{2,1,0:T(8,128)S(1)} %pack.1.own_ref), channel_id=1, source_target_pairs={{0,3},{1,2},{2,1},{3,0},{4,7},{5,6},{6,5},{7,4},{8,11},{9,10},{10,... | collective-permute-start | bytes 208904 | tf_op jit(solution)/shard_map/ppermute | solution.py:350
  22.8 0.0 collective-permute-start.2
  22.8 0.7 %collective-permute-start.1 = (f32[17,8,128]{2,1,0:T(8,128)S(1)}, f32[17,8,128]{2,1,0:T(8,128)S(1)}, u32[]{:S(2)}, u32[]{:S(2)}) collective-permute-start(f32[17,8,128]{2,1,0:T(8,128)S(1)} %pack.1.own_ref), channel_id=1, source_target_pairs={{0,1},{1,0},{2,3},{3,2},{4,5},{5,4},{6,7},{7,6},{8,9},{9,8},{10,11... | collective-permute-start | bytes 208904 | tf_op jit(solution)/shard_map/ppermute | solution.py:350
  23.5 1.3 %collective-permute-done.3.three_ref = f32[17,8,128]{2,1,0:T(8,128)S(1)} collective-permute-done((f32[17,8,128]{2,1,0:T(8,128)S(1)}, f32[17,8,128]{2,1,0:T(8,128)S(1)}, u32[]{:S(2)}, u32[]{:S(2)}) %collective-permute-start.3) | collective-permute-done | bytes 69664 | tf_op jit(solution)/shard_map/ppermute | solution.py:350
  24.8 2.8 %collective-permute-done.2.two_ref = f32[17,8,128]{2,1,0:T(8,128)S(1)} collective-permute-done((f32[17,8,128]{2,1,0:T(8,128)S(1)}, f32[17,8,128]{2,1,0:T(8,128)S(1)}, u32[]{:S(2)}, u32[]{:S(2)}) %collective-permute-start.2) | collective-permute-done | bytes 69664 | tf_op jit(solution)/shard_map/ppermute | solution.py:350
  27.6 0.0 collective-permute-done.1.one_ref
  27.6 0.0 copy-done
  27.6 3.0 %images.1 = (f32[8,8,128]{2,1,0:T(8,128)S(1)}, f32[8,8,128]{2,1,0:T(8,128)S(1)}, f32[32,128]{1,0:T(8,128)S(1)}) custom-call(f32[17,8,128]{2,1,0:T(8,128)S(1)} %pack.1.own_ref, f32[17,8,128]{2,1,0:T(8,128)S(1)} %collective-permute-done.1.one_ref, f32[17,8,128]{2,1,0:T(8,128)S(1)} %collective-permute-done.2.two_ref, ...), custom_call_target="tpu_custom_call" | custom-call | tf_op jit(solution)/shard_map/images/pallas_call | solution.py:351
  30.5 13.4 %all_to_all.23 = f32[32,1,128]{2,1,0:T(1,128)S(1)} all-to-all(f32[32,1,128]{2,1,0:T(1,128)S(1)} %bitcast.11), channel_id=1, replica_groups=mesh['scan'=8,'quad'=4,'place'=4] {'scan','quad'}, dimensions={0} | all-to-all | bytes 32768 | tf_op jit(solution)/shard_map/all_to_all | solution.py:367
  43.9 0.8 %last.1 = (f32[8,512]{1,0:T(8,128)}, f32[8,512]{1,0:T(8,128)}) custom-call(f32[32,128]{1,0:T(8,128)S(1)} %bitcast.10, f32[9,8,128]{2,1,0:T(8,128)S(1)} %combine.1.own_ref.fields_ref, f32[8,8,128]{2,1,0:T(8,128)S(1)} %get-tuple-element.6.first_ref, f32[8,8,128]{2,1,0:T(8,128)S(1)} %get-tuple-element.7.second_ref), custom_call_target="tpu_custom_call" | custom-call | tf_op jit(solution)/shard_map/last/pallas_call | solution.py:368
Async XLA Ops:
  2.1 11.4 %copy-start.1 = (s32[8,27]{1,0:T(8,128)S(1)}, s32[8,27]{1,0:T(8,128)}, u32[]{:S(2)}) copy-start(s32[8,27]{1,0:T(8,128)} %near_ref.1) | copy-start | bytes 2596
  13.6 13.9 %copy-start = (bf16[256,128]{1,0:T(8,128)(2,1)S(1)}, bf16[256,128]{1,0:T(8,128)(2,1)}, u32[]{:S(2)}) copy-start(bf16[256,128]{1,0:T(8,128)(2,1)} %constant.2.clone.table_ref) | copy-start | bytes 196612
  13.6 4.4 %collective-permute-start = (f32[9,8,128]{2,1,0:T(8,128)S(1)}, f32[9,8,128]{2,1,0:T(8,128)S(1)}, u32[]{:S(2)}, u32[]{:S(2)}) collective-permute-start(f32[9,8,128]{2,1,0:T(8,128)S(1)} %combine.1.own_ref.fields_ref), channel_id=1, source_target_pairs={{0,124},{1,125},{2,6},{3,7},{4,0},{5,1},{6,10},{7,11},{8,4},{9,5},... | collective-permute-start | bytes 110600 | tf_op jit(solution)/shard_map/ppermute | solution.py:340
  18.1 6.7 %collective-permute-start.3 = (f32[17,8,128]{2,1,0:T(8,128)S(1)}, f32[17,8,128]{2,1,0:T(8,128)S(1)}, u32[]{:S(2)}, u32[]{:S(2)}) collective-permute-start(f32[17,8,128]{2,1,0:T(8,128)S(1)} %pack.1.own_ref), channel_id=1, source_target_pairs={{0,3},{1,2},{2,1},{3,0},{4,7},{5,6},{6,5},{7,4},{8,11},{9,10},{10,... | collective-permute-start | bytes 208904 | tf_op jit(solution)/shard_map/ppermute | solution.py:350
  22.8 4.8 %collective-permute-start.2 = (f32[17,8,128]{2,1,0:T(8,128)S(1)}, f32[17,8,128]{2,1,0:T(8,128)S(1)}, u32[]{:S(2)}, u32[]{:S(2)}) collective-permute-start(f32[17,8,128]{2,1,0:T(8,128)S(1)} %pack.1.own_ref), channel_id=1, source_target_pairs={{0,2},{1,3},{2,0},{3,1},{4,6},{5,7},{6,4},{7,5},{8,10},{9,11},{10,... | collective-permute-start | bytes 208904 | tf_op jit(solution)/shard_map/ppermute | solution.py:350
  22.8 4.8 %collective-permute-start.1 = (f32[17,8,128]{2,1,0:T(8,128)S(1)}, f32[17,8,128]{2,1,0:T(8,128)S(1)}, u32[]{:S(2)}, u32[]{:S(2)}) collective-permute-start(f32[17,8,128]{2,1,0:T(8,128)S(1)} %pack.1.own_ref), channel_id=1, source_target_pairs={{0,1},{1,0},{2,3},{3,2},{4,5},{5,4},{6,7},{7,6},{8,9},{9,8},{10,11... | collective-permute-start | bytes 208904 | tf_op jit(solution)/shard_map/ppermute | solution.py:350

commit v5 on v4

--- a/solution.py
+++ b/solution.py
@@ -214,6 +214,7 @@
     next_ref,
     screen_ref,
     names_ref,
+    short_ref,
     index_ref,
     rows_ref,
     done_ref,
@@ -228,7 +229,14 @@
         tile = ref[2 * BLOCKS]
         names_ref[pl.ds(pl.multiple_of(inner, 8), 8), :] = local_names(tile, window_base())
         names_ref[pl.ds(pl.multiple_of(outer, 8), 8), :] = local_names(pltpu.roll(tile, 64, 1), window_base())
-    copy = pltpu.make_async_copy(names_ref.at[pl.ds(BLOCKS, 6 * BLOCKS)], index_ref, done_ref)
+    group = lax.broadcasted_iota(jnp.int32, (8, 128), 1) // 32
+    for half, members in ((0, (1, 2, 3, 4)), (1, (5, 6))):
+        tile = names_ref[8 * members[0] : 8 * members[0] + 8, :]
+        for slot, member in enumerate(members[1:], 1):
+            other = pltpu.roll(names_ref[8 * member : 8 * member + 8, :], 32 * slot, 1)
+            tile = jnp.where(group == slot, other, tile)
+        short_ref[8 * half : 8 * half + 8, :] = tile
+    copy = pltpu.make_async_copy(short_ref, index_ref, done_ref)
     copy.start()
     for ref, inner, outer in parts:
         for block in range(2 * BLOCKS):
@@ -243,10 +251,11 @@
     copy.wait()
 
     def near(block, offset):
-        return index_ref[block, offset]
+        device = block // BLOCKS
+        return index_ref[device // 4 * BLOCKS + block % BLOCKS, device % 4 * 32 + offset]
 
     def inside(block, offset):
-        return index_ref[BLOCKS + block, offset]
+        return near(BLOCKS + block, offset)
 
     coupled = couple(near, 6 * BLOCKS, wide_ref, rows_ref, table_ref)
     for block in range(6 * BLOCKS):
@@ -358,7 +367,8 @@
             pltpu.VMEM((8 * WINDOW + 8, 128), jnp.float32),
             pltpu.VMEM((8 * WINDOW, 128), jnp.float32),
             pltpu.VMEM((WINDOW, 128), jnp.int32),
-            pltpu.SMEM((6 * BLOCKS, 128), jnp.int32),
+            pltpu.VMEM((2 * BLOCKS, 128), jnp.int32),
+            pltpu.SMEM((2 * BLOCKS, 128), jnp.int32),
             pltpu.VMEM((6 * BLOCKS * 32, 256), jnp.bfloat16),
             pltpu.SemaphoreType.DMA,
         ],

time: 45 us -> 44.8 us (level)
  no operation moved by 1% of the time
where the time goes in v5:
time: 44.8 us; the launch traced here: 44.5 us
  blocking collectives  24.7 us (55%)
  starting transfers between devices  8.67 us (19%)
  Pallas kernels  5.24 us (12%)
  waiting for transfers between devices  5.16 us (12%)
  between operations  0.66 us (1%)
    all_to_all x1, blocking collectives, per_device(): sums = resident(lax.all_to_all(sums, ('scan', 'quad'), 0, 0, tiled=True))  13.4 us
    all_to_all x1, blocking collectives, per_device(): parts = resident(lax.all_to_all(parts, 'scan', 0, 0, tiled=True))  11.4 us
    ppermute x3, starting transfers between devices, per_device(): lax.ppermute(packed, 'place', [(i, i ^ step) for i in range(4)])  5.32 us
    ppermute x3, waiting for transfers between devices, per_device(): lax.ppermute(packed, 'place', [(i, i ^ step) for i in range(4)])  4.1 us
    ppermute x1, starting transfers between devices, per_device(): lax.ppermute(fields, ALL, [(i, (i - 4 if i % 4 < 2 else i + 4) % count) f...  3.35 us
    pallas_call x1, Pallas kernels, per_device(): pl.pallas_call(image_kernel, out_shape=(shape(BLOCKS, 8, 128), shape(BLOC...  2.79 us
    pallas_call x1, Pallas kernels, per_device(): pl.pallas_call(splat_kernel, out_shape=shape(8 * SHARE, 128), in_specs=sm...  1.5 us
    ppermute x1, waiting for transfers between devices, per_device(): lax.ppermute(fields, ALL, [(i, (i - 4 if i % 4 < 2 else i + 4) % count) f...  1.06 us
  transfers between devices with their start and end apart: 4, of which 3 were waited for; matrix products, arithmetic and copies ran while one was open for 0% of the time, Pallas kernels for 0%

profile of v5, /device:TPU:1, one launch (start us, length us, event | category | flops | bytes accessed | tf_op | source)
XLA Modules:
  0.0 44.5 jit_solution(2231723632637764649)
XLA Ops:
  0.6 1.5 %splat.1 = f32[320,128]{1,0:T(8,128)S(1)} custom-call(s32[16]{0:T(128)} %target_ref.1, f32[3,16,128]{2,1,0:T(8,128)} %bitcast.12, f32[3,16,128]{2,1,0:T(8,128)} %bitcast.13, f32[16,128]{1,0:T(8,128)} %weights_ref.1), custom_call_target="tpu_custom_call" | custom-call | tf_op jit(solution)/shard_map/splat/pallas_call | solution.py:330
  2.1 0.0 copy-start.1
  2.2 11.4 %all_to_all.22 = f32[8,40,128]{2,1,0:T(8,128)S(1)} all-to-all(f32[8,40,128]{2,1,0:T(8,128)S(1)} %bitcast.9), channel_id=1, replica_groups=mesh['scan'=8,'quad'=4,'place'=4] {'scan'}, dimensions={0} | all-to-all | bytes 327680 | tf_op jit(solution)/shard_map/all_to_all | solution.py:338
  13.5 0.0 copy-done.1
  13.5 0.1 combine.1.own_ref.fields_ref
  13.6 0.0 copy-start
  13.6 3.3 %collective-permute-start = (f32[9,8,128]{2,1,0:T(8,128)S(1)}, f32[9,8,128]{2,1,0:T(8,128)S(1)}, u32[]{:S(2)}, u32[]{:S(2)}) collective-permute-start(f32[9,8,128]{2,1,0:T(8,128)S(1)} %combine.1.own_ref.fields_ref), channel_id=1, source_target_pairs={{0,124},{1,125},{2,6},{3,7},{4,0},{5,1},{6,10},{7,11},{8,4},{9,5},... | collective-permute-start | bytes 110600 | tf_op jit(solution)/shard_map/ppermute | solution.py:349
  17.0 1.1 %collective-permute-done.beside_ref = f32[9,8,128]{2,1,0:T(8,128)S(1)} collective-permute-done((f32[9,8,128]{2,1,0:T(8,128)S(1)}, f32[9,8,128]{2,1,0:T(8,128)S(1)}, u32[]{:S(2)}, u32[]{:S(2)}) %collective-permute-start) | collective-permute-done | bytes 36896 | tf_op jit(solution)/shard_map/ppermute | solution.py:349
  18.1 0.1 pack.1.own_ref
  18.1 4.7 %collective-permute-start.3 = (f32[17,8,128]{2,1,0:T(8,128)S(1)}, f32[17,8,128]{2,1,0:T(8,128)S(1)}, u32[]{:S(2)}, u32[]{:S(2)}) collective-permute-start(f32[17,8,128]{2,1,0:T(8,128)S(1)} %pack.1.own_ref), channel_id=1, source_target_pairs={{0,3},{1,2},{2,1},{3,0},{4,7},{5,6},{6,5},{7,4},{8,11},{9,10},{10,... | collective-permute-start | bytes 208904 | tf_op jit(solution)/shard_map/ppermute | solution.py:359
  22.8 0.0 collective-permute-start.2
  22.8 0.7 %collective-permute-start.1 = (f32[17,8,128]{2,1,0:T(8,128)S(1)}, f32[17,8,128]{2,1,0:T(8,128)S(1)}, u32[]{:S(2)}, u32[]{:S(2)}) collective-permute-start(f32[17,8,128]{2,1,0:T(8,128)S(1)} %pack.1.own_ref), channel_id=1, source_target_pairs={{0,1},{1,0},{2,3},{3,2},{4,5},{5,4},{6,7},{7,6},{8,9},{9,8},{10,11... | collective-permute-start | bytes 208904 | tf_op jit(solution)/shard_map/ppermute | solution.py:359
  23.5 1.3 %collective-permute-done.3.three_ref = f32[17,8,128]{2,1,0:T(8,128)S(1)} collective-permute-done((f32[17,8,128]{2,1,0:T(8,128)S(1)}, f32[17,8,128]{2,1,0:T(8,128)S(1)}, u32[]{:S(2)}, u32[]{:S(2)}) %collective-permute-start.3) | collective-permute-done | bytes 69664 | tf_op jit(solution)/shard_map/ppermute | solution.py:359
  24.8 2.8 %collective-permute-done.2.two_ref = f32[17,8,128]{2,1,0:T(8,128)S(1)} collective-permute-done((f32[17,8,128]{2,1,0:T(8,128)S(1)}, f32[17,8,128]{2,1,0:T(8,128)S(1)}, u32[]{:S(2)}, u32[]{:S(2)}) %collective-permute-start.2) | collective-permute-done | bytes 69664 | tf_op jit(solution)/shard_map/ppermute | solution.py:359
  27.6 0.0 collective-permute-done.1.one_ref
  27.6 0.0 copy-done
  27.6 2.8 %images.1 = (f32[8,8,128]{2,1,0:T(8,128)S(1)}, f32[8,8,128]{2,1,0:T(8,128)S(1)}, f32[32,128]{1,0:T(8,128)S(1)}) custom-call(f32[17,8,128]{2,1,0:T(8,128)S(1)} %pack.1.own_ref, f32[17,8,128]{2,1,0:T(8,128)S(1)} %collective-permute-done.1.one_ref, f32[17,8,128]{2,1,0:T(8,128)S(1)} %collective-permute-done.2.two_ref, ...), custom_call_target="tpu_custom_call" | custom-call | tf_op jit(solution)/shard_map/images/pallas_call | solution.py:360
  30.4 13.4 %all_to_all.23 = f32[32,1,128]{2,1,0:T(1,128)S(1)} all-to-all(f32[32,1,128]{2,1,0:T(1,128)S(1)} %bitcast.11), channel_id=1, replica_groups=mesh['scan'=8,'quad'=4,'place'=4] {'scan','quad'}, dimensions={0} | all-to-all | bytes 32768 | tf_op jit(solution)/shard_map/all_to_all | solution.py:377
  43.7 0.8 %last.1 = (f32[8,512]{1,0:T(8,128)}, f32[8,512]{1,0:T(8,128)}) custom-call(f32[32,128]{1,0:T(8,128)S(1)} %bitcast.10, f32[9,8,128]{2,1,0:T(8,128)S(1)} %combine.1.own_ref.fields_ref, f32[8,8,128]{2,1,0:T(8,128)S(1)} %get-tuple-element.6.first_ref, f32[8,8,128]{2,1,0:T(8,128)S(1)} %get-tuple-element.7.second_ref), custom_call_target="tpu_custom_call" | custom-call | tf_op jit(solution)/shard_map/last/pallas_call | solution.py:378
Async XLA Ops:
  2.1 11.4 %copy-start.1 = (s32[8,27]{1,0:T(8,128)S(1)}, s32[8,27]{1,0:T(8,128)}, u32[]{:S(2)}) copy-start(s32[8,27]{1,0:T(8,128)} %near_ref.1) | copy-start | bytes 2596
  13.6 13.9 %copy-start = (bf16[256,128]{1,0:T(8,128)(2,1)S(1)}, bf16[256,128]{1,0:T(8,128)(2,1)}, u32[]{:S(2)}) copy-start(bf16[256,128]{1,0:T(8,128)(2,1)} %constant.2.clone.table_ref) | copy-start | bytes 196612
  13.6 4.4 %collective-permute-start = (f32[9,8,128]{2,1,0:T(8,128)S(1)}, f32[9,8,128]{2,1,0:T(8,128)S(1)}, u32[]{:S(2)}, u32[]{:S(2)}) collective-permute-start(f32[9,8,128]{2,1,0:T(8,128)S(1)} %combine.1.own_ref.fields_ref), channel_id=1, source_target_pairs={{0,124},{1,125},{2,6},{3,7},{4,0},{5,1},{6,10},{7,11},{8,4},{9,5},... | collective-permute-start | bytes 110600 | tf_op jit(solution)/shard_map/ppermute | solution.py:349
  18.1 6.7 %collective-permute-start.3 = (f32[17,8,128]{2,1,0:T(8,128)S(1)}, f32[17,8,128]{2,1,0:T(8,128)S(1)}, u32[]{:S(2)}, u32[]{:S(2)}) collective-permute-start(f32[17,8,128]{2,1,0:T(8,128)S(1)} %pack.1.own_ref), channel_id=1, source_target_pairs={{0,3},{1,2},{2,1},{3,0},{4,7},{5,6},{6,5},{7,4},{8,11},{9,10},{10,... | collective-permute-start | bytes 208904 | tf_op jit(solution)/shard_map/ppermute | solution.py:359
  22.8 4.8 %collective-permute-start.2 = (f32[17,8,128]{2,1,0:T(8,128)S(1)}, f32[17,8,128]{2,1,0:T(8,128)S(1)}, u32[]{:S(2)}, u32[]{:S(2)}) collective-permute-start(f32[17,8,128]{2,1,0:T(8,128)S(1)} %pack.1.own_ref), channel_id=1, source_target_pairs={{0,2},{1,3},{2,0},{3,1},{4,6},{5,7},{6,4},{7,5},{8,10},{9,11},{10,... | collective-permute-start | bytes 208904 | tf_op jit(solution)/shard_map/ppermute | solution.py:359
  22.8 4.8 %collective-permute-start.1 = (f32[17,8,128]{2,1,0:T(8,128)S(1)}, f32[17,8,128]{2,1,0:T(8,128)S(1)}, u32[]{:S(2)}, u32[]{:S(2)}) collective-permute-start(f32[17,8,128]{2,1,0:T(8,128)S(1)} %pack.1.own_ref), channel_id=1, source_target_pairs={{0,1},{1,0},{2,3},{3,2},{4,5},{5,4},{6,7},{7,6},{8,9},{9,8},{10,11... | collective-permute-start | bytes 208904 | tf_op jit(solution)/shard_map/ppermute | solution.py:359

commit v6 on v5

--- a/solution.py
+++ b/solution.py
@@ -127,11 +127,16 @@
     out_ref[BLOCKS, :, 0:27] = near_ref[...].astype(jnp.float32)
 
 
-def pack_kernel(own_ref, beside_ref, out_ref):
+def pack_kernel(own_ref, beside_ref, out_ref, longer_ref):
+    longer_ref[2 * BLOCKS + 1] = own_ref[BLOCKS]
     for block in range(BLOCKS):
         out_ref[block] = own_ref[block]
         out_ref[BLOCKS + block] = beside_ref[block]
-    out_ref[2 * BLOCKS] = jnp.where(left_half(), own_ref[BLOCKS], pltpu.roll(beside_ref[BLOCKS], 64, 1))
+        longer_ref[block] = own_ref[block]
+        longer_ref[BLOCKS + block] = beside_ref[block]
+    tables = jnp.where(left_half(), own_ref[BLOCKS], pltpu.roll(beside_ref[BLOCKS], 64, 1))
+    out_ref[2 * BLOCKS] = tables
+    longer_ref[2 * BLOCKS] = tables
 
 
 def doubled(tile, first_half):
@@ -347,16 +352,17 @@
     )
     count = lax.axis_size("scan") * lax.axis_size("quad") * 4
     beside = resident(lax.ppermute(fields, ALL, [(i, (i - 4 if i % 4 < 2 else i + 4) % count) for i in range(count)]))
-    packed = resident(
-        pl.pallas_call(
-            pack_kernel,
-            out_shape=shape(2 * BLOCKS + 1, 8, 128),
-            in_specs=vmem(2),
-            out_specs=vmem(1)[0],
-            name="pack",
-        )(fields, beside)
-    )
-    others = [resident(lax.ppermute(packed, "place", [(i, i ^ step) for i in range(4)])) for step in (1, 2, 3)]
+    packed, longer = pl.pallas_call(
+        pack_kernel,
+        out_shape=(shape(2 * BLOCKS + 1, 8, 128), shape(2 * BLOCKS + 2, 8, 128)),
+        in_specs=vmem(2),
+        out_specs=tuple(vmem(2)),
+        name="pack",
+    )(fields, beside)
+    others = [
+        resident(lax.ppermute(longer if step == 2 else packed, "place", [(i, i ^ step) for i in range(4)]))
+        for step in (1, 2, 3)
+    ]
     first, second, sums = pl.pallas_call(
         image_kernel,
         out_shape=(shape(BLOCKS, 8, 128), shape(BLOCKS, 8, 128), shape(32, 128)),
@@ -373,7 +379,7 @@
             pltpu.SemaphoreType.DMA,
         ],
         name="images",
-    )(packed, *others, table)
+    )(resident(packed), *others, table)
     sums = resident(lax.all_to_all(sums, ("scan", "quad"), 0, 0, tiled=True))
     return pl.pallas_call(
         last_kernel,

time: 44.8 us -> 44.3 us (0.989)
  blocking collectives: 24.7 us -> 24.1 us
    all_to_all x1, blocking collectives: 13.4 us -> 12.8 us  [per_device(): sums = resident(lax.all_to_all(sums, ('scan', 'quad'), 0, 0, tiled=True))]
  transfers between devices with their start and end apart: 4 -> 4, of which waited for: 3 -> 2; matrix products, arithmetic and copies ran while one was open for 0% -> 0% of each run, Pallas kernels for 0% -> 0%
where the time goes in v6:
time: 44.3 us; the launch traced here: 44.1 us
  blocking collectives  24.1 us (54%)
  starting transfers between devices  8.58 us (19%)
  waiting for transfers between devices  5.4 us (12%)
  Pallas kernels  5.24 us (12%)
  between operations  0.67 us (2%)
    all_to_all x1, blocking collectives, per_device(): sums = resident(lax.all_to_all(sums, ('scan', 'quad'), 0, 0, tiled=True))  12.8 us
    all_to_all x1, blocking collectives, per_device(): parts = resident(lax.all_to_all(parts, 'scan', 0, 0, tiled=True))  11.4 us
    ppermute x3, starting transfers between devices, per_device(): lax.ppermute(longer if step == 2 else packed, 'place', [(i, i ^ step) for...  5.23 us
    ppermute x3, waiting for transfers between devices, per_device(): lax.ppermute(longer if step == 2 else packed, 'place', [(i, i ^ step) for...  4.34 us
    ppermute x1, starting transfers between devices, per_device(): lax.ppermute(fields, ALL, [(i, (i - 4 if i % 4 < 2 else i + 4) % count) f...  3.35 us
    pallas_call x1, Pallas kernels, per_device(): pl.pallas_call(image_kernel, out_shape=(shape(BLOCKS, 8, 128), shape(BLOC...  2.79 us
    pallas_call x1, Pallas kernels, per_device(): pl.pallas_call(splat_kernel, out_shape=shape(8 * SHARE, 128), in_specs=sm...  1.5 us
    ppermute x1, waiting for transfers between devices, per_device(): lax.ppermute(fields, ALL, [(i, (i - 4 if i % 4 < 2 else i + 4) % count) f...  1.06 us
  transfers between devices with their start and end apart: 4, of which 2 were waited for; matrix products, arithmetic and copies ran while one was open for 0% of the time, Pallas kernels for 0%

profile of v6, /device:TPU:1, one launch (start us, length us, event | category | flops | bytes accessed | tf_op | source)
XLA Modules:
  0.0 44.1 jit_solution(10732680257664587242)
XLA Ops:
  0.6 1.5 %splat.1 = f32[320,128]{1,0:T(8,128)S(1)} custom-call(s32[16]{0:T(128)} %target_ref.1, f32[3,16,128]{2,1,0:T(8,128)} %bitcast.12, f32[3,16,128]{2,1,0:T(8,128)} %bitcast.13, f32[16,128]{1,0:T(8,128)} %weights_ref.1), custom_call_target="tpu_custom_call" | custom-call | tf_op jit(solution)/shard_map/splat/pallas_call | solution.py:335
  2.1 0.0 copy-start.1
  2.2 11.4 %all_to_all.22 = f32[8,40,128]{2,1,0:T(8,128)S(1)} all-to-all(f32[8,40,128]{2,1,0:T(8,128)S(1)} %bitcast.9), channel_id=1, replica_groups=mesh['scan'=8,'quad'=4,'place'=4] {'scan'}, dimensions={0} | all-to-all | bytes 327680 | tf_op jit(solution)/shard_map/all_to_all | solution.py:343
  13.5 0.0 copy-done.1
  13.5 0.1 combine.1.own_ref.fields_ref
  13.6 0.0 copy-start
  13.6 3.3 %collective-permute-start = (f32[9,8,128]{2,1,0:T(8,128)S(1)}, f32[9,8,128]{2,1,0:T(8,128)S(1)}, u32[]{:S(2)}, u32[]{:S(2)}) collective-permute-start(f32[9,8,128]{2,1,0:T(8,128)S(1)} %combine.1.own_ref.fields_ref), channel_id=1, source_target_pairs={{0,124},{1,125},{2,6},{3,7},{4,0},{5,1},{6,10},{7,11},{8,4},{9,5},... | collective-permute-start | bytes 110600 | tf_op jit(solution)/shard_map/ppermute | solution.py:354
  17.0 1.1 %collective-permute-done.beside_ref = f32[9,8,128]{2,1,0:T(8,128)S(1)} collective-permute-done((f32[9,8,128]{2,1,0:T(8,128)S(1)}, f32[9,8,128]{2,1,0:T(8,128)S(1)}, u32[]{:S(2)}, u32[]{:S(2)}) %collective-permute-start) | collective-permute-done | bytes 36896 | tf_op jit(solution)/shard_map/ppermute | solution.py:354
  18.1 0.1 pack.1
  18.1 4.5 %collective-permute-start.2 = (f32[18,8,128]{2,1,0:T(8,128)S(1)}, f32[18,8,128]{2,1,0:T(8,128)S(1)}, u32[]{:S(2)}, u32[]{:S(2)}) collective-permute-start(f32[18,8,128]{2,1,0:T(8,128)S(1)} %get-tuple-element.8), channel_id=1, source_target_pairs={{0,2},{1,3},{2,0},{3,1},{4,6},{5,7},{6,4},{7,5},{8,10},{9,11},{10,... | collective-permute-start | bytes 221192 | tf_op jit(solution)/shard_map/ppermute | solution.py:363
  22.6 0.3 collective-permute-start.3
  22.9 0.5 %collective-permute-start.1 = (f32[17,8,128]{2,1,0:T(8,128)S(1)}, f32[17,8,128]{2,1,0:T(8,128)S(1)}, u32[]{:S(2)}, u32[]{:S(2)}) collective-permute-start(f32[17,8,128]{2,1,0:T(8,128)S(1)} %get-tuple-element.7.own_ref), channel_id=1, source_target_pairs={{0,1},{1,0},{2,3},{3,2},{4,5},{5,4},{6,7},{7,6},{8,9},{9,8},{10,11... | collective-permute-start | bytes 208904 | tf_op jit(solution)/shard_map/ppermute | solution.py:363
  23.4 4.3 %collective-permute-done.3.three_ref = f32[17,8,128]{2,1,0:T(8,128)S(1)} collective-permute-done((f32[17,8,128]{2,1,0:T(8,128)S(1)}, f32[17,8,128]{2,1,0:T(8,128)S(1)}, u32[]{:S(2)}, u32[]{:S(2)}) %collective-permute-start.3) | collective-permute-done | bytes 69664 | tf_op jit(solution)/shard_map/ppermute | solution.py:363
  27.7 0.0 collective-permute-done.1.one_ref
  27.7 0.0 collective-permute-done.2.two_ref
  27.7 0.0 copy-done
  27.7 2.8 %images.1 = (f32[8,8,128]{2,1,0:T(8,128)S(1)}, f32[8,8,128]{2,1,0:T(8,128)S(1)}, f32[32,128]{1,0:T(8,128)S(1)}) custom-call(f32[17,8,128]{2,1,0:T(8,128)S(1)} %get-tuple-element.7.own_ref, f32[17,8,128]{2,1,0:T(8,128)S(1)} %collective-permute-done.1.one_ref, f32[18,8,128]{2,1,0:T(8,128)S(1)} %collective-permute-done.2.two_ref, ...), custom_call_target="tpu_custom_call" | custom-call | tf_op jit(solution)/shard_map/images/pallas_call | solution.py:366
  30.5 12.8 %all_to_all.23 = f32[32,1,128]{2,1,0:T(1,128)S(1)} all-to-all(f32[32,1,128]{2,1,0:T(1,128)S(1)} %bitcast.11), channel_id=1, replica_groups=mesh['scan'=8,'quad'=4,'place'=4] {'scan','quad'}, dimensions={0} | all-to-all | bytes 32768 | tf_op jit(solution)/shard_map/all_to_all | solution.py:383
  43.3 0.8 %last.1 = (f32[8,512]{1,0:T(8,128)}, f32[8,512]{1,0:T(8,128)}) custom-call(f32[32,128]{1,0:T(8,128)S(1)} %bitcast.10, f32[9,8,128]{2,1,0:T(8,128)S(1)} %combine.1.own_ref.fields_ref, f32[8,8,128]{2,1,0:T(8,128)S(1)} %get-tuple-element.10.first_ref, f32[8,8,128]{2,1,0:T(8,128)S(1)} %get-tuple-element.11.second_ref), custom_call_target="tpu_custom_call" | custom-call | tf_op jit(solution)/shard_map/last/pallas_call | solution.py:384
Async XLA Ops:
  2.1 11.4 %copy-start.1 = (s32[8,27]{1,0:T(8,128)S(1)}, s32[8,27]{1,0:T(8,128)}, u32[]{:S(2)}) copy-start(s32[8,27]{1,0:T(8,128)} %near_ref.1) | copy-start | bytes 2596
  13.6 14.1 %copy-start = (bf16[256,128]{1,0:T(8,128)(2,1)S(1)}, bf16[256,128]{1,0:T(8,128)(2,1)}, u32[]{:S(2)}) copy-start(bf16[256,128]{1,0:T(8,128)(2,1)} %constant.2.clone.table_ref) | copy-start | bytes 196612
  13.6 4.4 %collective-permute-start = (f32[9,8,128]{2,1,0:T(8,128)S(1)}, f32[9,8,128]{2,1,0:T(8,128)S(1)}, u32[]{:S(2)}, u32[]{:S(2)}) collective-permute-start(f32[9,8,128]{2,1,0:T(8,128)S(1)} %combine.1.own_ref.fields_ref), channel_id=1, source_target_pairs={{0,124},{1,125},{2,6},{3,7},{4,0},{5,1},{6,10},{7,11},{8,4},{9,5},... | collective-permute-start | bytes 110600 | tf_op jit(solution)/shard_map/ppermute | solution.py:354
  18.1 9.6 %collective-permute-start.2 = (f32[18,8,128]{2,1,0:T(8,128)S(1)}, f32[18,8,128]{2,1,0:T(8,128)S(1)}, u32[]{:S(2)}, u32[]{:S(2)}) collective-permute-start(f32[18,8,128]{2,1,0:T(8,128)S(1)} %get-tuple-element.8), channel_id=1, source_target_pairs={{0,2},{1,3},{2,0},{3,1},{4,6},{5,7},{6,4},{7,5},{8,10},{9,11},{10,... | collective-permute-start | bytes 221192 | tf_op jit(solution)/shard_map/ppermute | solution.py:363
  22.6 5.1 %collective-permute-start.3 = (f32[17,8,128]{2,1,0:T(8,128)S(1)}, f32[17,8,128]{2,1,0:T(8,128)S(1)}, u32[]{:S(2)}, u32[]{:S(2)}) collective-permute-start(f32[17,8,128]{2,1,0:T(8,128)S(1)} %get-tuple-element.7.own_ref), channel_id=1, source_target_pairs={{0,3},{1,2},{2,1},{3,0},{4,7},{5,6},{6,5},{7,4},{8,11},{9,10},{10,... | collective-permute-start | bytes 208904 | tf_op jit(solution)/shard_map/ppermute | solution.py:363
  22.9 4.8 %collective-permute-start.1 = (f32[17,8,128]{2,1,0:T(8,128)S(1)}, f32[17,8,128]{2,1,0:T(8,128)S(1)}, u32[]{:S(2)}, u32[]{:S(2)}) collective-permute-start(f32[17,8,128]{2,1,0:T(8,128)S(1)} %get-tuple-element.7.own_ref), channel_id=1, source_target_pairs={{0,1},{1,0},{2,3},{3,2},{4,5},{5,4},{6,7},{7,6},{8,9},{9,8},{10,11... | collective-permute-start | bytes 208904 | tf_op jit(solution)/shard_map/ppermute | solution.py:363

commit v7 on v6

--- a/solution.py
+++ b/solution.py
@@ -10,7 +10,8 @@
 SCREEN = 16.0
 BLOCKS = 8
 SLOTS = 4
-SHARE = SLOTS * 8 + 8
+SHARE = SLOTS * 8 + 1
+ROOM = SLOTS * 8 + 8
 ALL = ("scan", "quad", "place")
 WINDOW = 8 * BLOCKS
 
@@ -49,13 +50,13 @@
     return lax.broadcasted_iota(jnp.int32, (8, 128), 1) < 64
 
 
-def splat_kernel(target_ref, spots_ref, norms_ref, weights_ref, out_ref, used_ref):
+def splat_kernel(target_ref, spots_ref, norms_ref, weights_ref, out_ref, used_ref, work_ref):
     node = lax.broadcasted_iota(jnp.int32, (8, 128), 0).astype(jnp.float32)
     first_half = left_half()
     nothing = jnp.zeros((64, 128), jnp.float32)
     for row in range(8):
         used_ref[row] = 0
-        out_ref[row * SHARE + SLOTS * 8 : (row + 1) * SHARE, :] = jnp.full((8, 128), -1.0, jnp.float32)
+        work_ref[row * ROOM + SLOTS * 8 : (row + 1) * ROOM, :] = jnp.full((8, 128), -1.0, jnp.float32)
     for q in range(16):
         hats, slopes = [], []
         for dim in range(3):
@@ -95,10 +96,18 @@
         row = target // (16 * BLOCKS)
         slot = used_ref[row]
         used_ref[row] = slot + 1
-        place = pl.multiple_of(row * SHARE + slot * 8, 8)
-        out_ref[pl.ds(place, 8), :] = jnp.where(first_half, total[:8], total[8:])
+        place = pl.multiple_of(row * ROOM + slot * 8, 8)
+        work_ref[pl.ds(place, 8), :] = jnp.where(first_half, total[:8], total[8:])
         block = (target % BLOCKS).astype(jnp.float32)
-        out_ref[pl.ds(row * SHARE + SLOTS * 8 + slot, 1), :] = jnp.full((1, 128), block, jnp.float32)
+        work_ref[pl.ds(row * ROOM + SLOTS * 8 + slot, 1), :] = jnp.full((1, 128), block, jnp.float32)
+    group = lax.broadcasted_iota(jnp.int32, (1, 128), 1) // 32
+    for row in range(8):
+        at = row * ROOM + SLOTS * 8
+        out_ref[row * SHARE : row * SHARE + SLOTS * 8, :] = work_ref[row * ROOM : at, :]
+        names = work_ref[at : at + 1, :]
+        for slot in range(1, SLOTS):
+            names = jnp.where(group == slot, work_ref[at + slot : at + slot + 1, :], names)
+        out_ref[row * SHARE + SLOTS * 8 : (row + 1) * SHARE, :] = names
 
 
 def local_names(table, base):
@@ -115,10 +124,11 @@
 def combine_kernel(parts_ref, near_ref, out_ref):
     sums = [jnp.zeros((8, 128), jnp.float32) for _ in range(BLOCKS)]
     for source in range(8):
+        at = source * SHARE
+        names = parts_ref[at + SLOTS * 8 : at + SHARE, :]
         for slot in range(SLOTS):
-            at = source * SHARE
             part = parts_ref[at + slot * 8 : at + slot * 8 + 8, :]
-            name = jnp.broadcast_to(parts_ref[at + SLOTS * 8 + slot : at + SLOTS * 8 + slot + 1, :], (8, 128))
+            name = jnp.broadcast_to(names[:, 32 * slot : 32 * slot + 1], (8, 128))
             for block in range(BLOCKS):
                 sums[block] = sums[block] + jnp.where(name == float(block), part, 0.0)
     for block in range(BLOCKS):
@@ -182,16 +192,15 @@
             [jnp.concatenate([here[half], ends[half]], axis=0) for half in range(2)], axis=1
         )
         high, low = split(rows)
-        rows_ref[16 * block : 16 * block + 16, :] = high
-        rows_ref[16 * (blocks + block) : 16 * (blocks + block) + 16, :] = low
-    both = jnp.dot(rows_ref[0 : 32 * blocks, :], table_ref[...], preferred_element_type=jnp.float32)
+        rows_ref[16 * block : 16 * block + 16, 0:256] = high
+        rows_ref[16 * block : 16 * block + 16, 256:512] = low
+    sums = jnp.dot(rows_ref[0 : 16 * blocks, :], table_ref[...], preferred_element_type=jnp.float32)
     centre = jnp.where(first_half, 2.0 / 36.0, 4.0 / 36.0)
     side = jnp.where(first_half, -1.0 / 36.0, 1.0 / 36.0)
     result = []
     for block in range(blocks):
-        at, other = 16 * block, 16 * (blocks + block)
-        here = both[at : at + 8] + both[other : other + 8]
-        ends = both[at + 8 : at + 16] + both[other + 8 : other + 16]
+        here = sums[16 * block : 16 * block + 8]
+        ends = sums[16 * block + 8 : 16 * block + 16]
         before = pltpu.roll(jnp.where(bottom, ends, here), 1, 0)
         after = pltpu.roll(jnp.where(top, ends, here), 7, 0)
         value = centre * here + side * (before + after)
@@ -331,16 +340,17 @@
 
 
 def per_device(positions, normals, weights, point_target, neighbours):
-    table = resident(jnp.asarray(plane_table(), jnp.bfloat16))
+    table = resident(jnp.asarray(np.concatenate([plane_table()] * 2), jnp.bfloat16))
     parts = pl.pallas_call(
         splat_kernel,
         out_shape=shape(8 * SHARE, 128),
         in_specs=smem(1) + vmem(3),
         out_specs=vmem(1)[0],
-        scratch_shapes=[pltpu.SMEM((8,), jnp.int32)],
+        scratch_shapes=[pltpu.SMEM((8,), jnp.int32), pltpu.VMEM((8 * ROOM, 128), jnp.float32)],
         name="splat",
     )(point_target, positions.transpose(1, 0, 2), normals.transpose(1, 0, 2), weights)
-    parts = resident(lax.all_to_all(parts, "scan", 0, 0, tiled=True))
+    parts = lax.all_to_all(parts.reshape(8, 1, SHARE * 128), "scan", 0, 0, tiled=True)
+    parts = resident(parts.reshape(8 * SHARE, 128))
     fields = resident(
         pl.pallas_call(
             combine_kernel,
@@ -375,7 +385,7 @@
             pltpu.VMEM((WINDOW, 128), jnp.int32),
             pltpu.VMEM((2 * BLOCKS, 128), jnp.int32),
             pltpu.SMEM((2 * BLOCKS, 128), jnp.int32),
-            pltpu.VMEM((6 * BLOCKS * 32, 256), jnp.bfloat16),
+            pltpu.VMEM((6 * BLOCKS * 16, 512), jnp.bfloat16),
             pltpu.SemaphoreType.DMA,
         ],
         name="images",

time: 44.3 us -> 44.1 us (level)
  no operation moved by 1% of the time
where the time goes in v7:
time: 44.1 us; the launch traced here: 43.8 us
  blocking collectives  23.9 us (54%)
  starting transfers between devices  8.55 us (19%)
  waiting for transfers between devices  5.39 us (12%)
  Pallas kernels  5.32 us (12%)
  between operations  0.67 us (2%)
    all_to_all x1, blocking collectives, per_device(): sums = resident(lax.all_to_all(sums, ('scan', 'quad'), 0, 0, tiled=True))  12.8 us
    all_to_all x1, blocking collectives, per_device(): lax.all_to_all(parts.reshape(8, 1, SHARE * 128), 'scan', 0, 0, tiled=True)  11.1 us
    ppermute x3, starting transfers between devices, per_device(): lax.ppermute(longer if step == 2 else packed, 'place', [(i, i ^ step) for...  5.24 us
    ppermute x3, waiting for transfers between devices, per_device(): lax.ppermute(longer if step == 2 else packed, 'place', [(i, i ^ step) for...  4.33 us
    ppermute x1, starting transfers between devices, per_device(): lax.ppermute(fields, ALL, [(i, (i - 4 if i % 4 < 2 else i + 4) % count) f...  3.31 us
    pallas_call x1, Pallas kernels, per_device(): pl.pallas_call(image_kernel, out_shape=(shape(BLOCKS, 8, 128), shape(BLOC...  2.74 us
    pallas_call x1, Pallas kernels, per_device(): pl.pallas_call(splat_kernel, out_shape=shape(8 * SHARE, 128), in_specs=sm...  1.54 us
    ppermute x1, waiting for transfers between devices, per_device(): lax.ppermute(fields, ALL, [(i, (i - 4 if i % 4 < 2 else i + 4) % count) f...  1.06 us
  transfers between devices with their start and end apart: 4, of which 2 were waited for; matrix products, arithmetic and copies ran while one was open for 0% of the time, Pallas kernels for 0%

profile of v7, /device:TPU:1, one launch (start us, length us, event | category | flops | bytes accessed | tf_op | source)
XLA Modules:
  0.0 43.8 jit_solution(16030588150029738778)
XLA Ops:
  0.6 1.5 %splat.1 = f32[264,128]{1,0:T(8,128)S(1)} custom-call(s32[16]{0:T(128)} %target_ref.1, f32[3,16,128]{2,1,0:T(8,128)} %bitcast.12, f32[3,16,128]{2,1,0:T(8,128)} %bitcast.13, f32[16,128]{1,0:T(8,128)} %weights_ref.1), custom_call_target="tpu_custom_call" | custom-call | tf_op jit(solution)/shard_map/splat/pallas_call | solution.py:344
  2.2 0.0 copy-start.1
  2.2 11.1 %all_to_all.16 = f32[8,1,4224]{2,1,0:T(1,128)S(1)} all-to-all(f32[8,1,4224]{2,1,0:T(1,128)S(1)} %bitcast.9), channel_id=1, replica_groups=mesh['scan'=8,'quad'=4,'place'=4] {'scan'}, dimensions={0} | all-to-all | bytes 270336 | tf_op jit(solution)/shard_map/all_to_all | solution.py:352
  13.3 0.0 copy-start
  13.3 0.0 copy-done.1
  13.3 0.2 combine.1.own_ref.fields_ref
  13.5 3.3 %collective-permute-start = (f32[9,8,128]{2,1,0:T(8,128)S(1)}, f32[9,8,128]{2,1,0:T(8,128)S(1)}, u32[]{:S(2)}, u32[]{:S(2)}) collective-permute-start(f32[9,8,128]{2,1,0:T(8,128)S(1)} %combine.1.own_ref.fields_ref), channel_id=1, source_target_pairs={{0,124},{1,125},{2,6},{3,7},{4,0},{5,1},{6,10},{7,11},{8,4},{9,5},... | collective-permute-start | bytes 110600 | tf_op jit(solution)/shard_map/ppermute | solution.py:364
  16.8 1.1 %collective-permute-done.beside_ref = f32[9,8,128]{2,1,0:T(8,128)S(1)} collective-permute-done((f32[9,8,128]{2,1,0:T(8,128)S(1)}, f32[9,8,128]{2,1,0:T(8,128)S(1)}, u32[]{:S(2)}, u32[]{:S(2)}) %collective-permute-start) | collective-permute-done | bytes 36896 | tf_op jit(solution)/shard_map/ppermute | solution.py:364
  17.9 0.1 pack.1
  17.9 4.5 %collective-permute-start.2 = (f32[18,8,128]{2,1,0:T(8,128)S(1)}, f32[18,8,128]{2,1,0:T(8,128)S(1)}, u32[]{:S(2)}, u32[]{:S(2)}) collective-permute-start(f32[18,8,128]{2,1,0:T(8,128)S(1)} %get-tuple-element.8), channel_id=1, source_target_pairs={{0,2},{1,3},{2,0},{3,1},{4,6},{5,7},{6,4},{7,5},{8,10},{9,11},{10,... | collective-permute-start | bytes 221192 | tf_op jit(solution)/shard_map/ppermute | solution.py:373
  22.4 0.3 collective-permute-start.3
  22.7 0.5 %collective-permute-start.1 = (f32[17,8,128]{2,1,0:T(8,128)S(1)}, f32[17,8,128]{2,1,0:T(8,128)S(1)}, u32[]{:S(2)}, u32[]{:S(2)}) collective-permute-start(f32[17,8,128]{2,1,0:T(8,128)S(1)} %get-tuple-element.7.own_ref), channel_id=1, source_target_pairs={{0,1},{1,0},{2,3},{3,2},{4,5},{5,4},{6,7},{7,6},{8,9},{9,8},{10,11... | collective-permute-start | bytes 208904 | tf_op jit(solution)/shard_map/ppermute | solution.py:373
  23.2 4.3 %collective-permute-done.3.three_ref = f32[17,8,128]{2,1,0:T(8,128)S(1)} collective-permute-done((f32[17,8,128]{2,1,0:T(8,128)S(1)}, f32[17,8,128]{2,1,0:T(8,128)S(1)}, u32[]{:S(2)}, u32[]{:S(2)}) %collective-permute-start.3) | collective-permute-done | bytes 69664 | tf_op jit(solution)/shard_map/ppermute | solution.py:373
  27.5 0.0 collective-permute-done.1.one_ref
  27.5 0.0 collective-permute-done.2.two_ref
  27.5 0.0 copy-done
  27.5 2.7 %images.1 = (f32[8,8,128]{2,1,0:T(8,128)S(1)}, f32[8,8,128]{2,1,0:T(8,128)S(1)}, f32[32,128]{1,0:T(8,128)S(1)}) custom-call(f32[17,8,128]{2,1,0:T(8,128)S(1)} %get-tuple-element.7.own_ref, f32[17,8,128]{2,1,0:T(8,128)S(1)} %collective-permute-done.1.one_ref, f32[18,8,128]{2,1,0:T(8,128)S(1)} %collective-permute-done.2.two_ref, ...), custom_call_target="tpu_custom_call" | custom-call | tf_op jit(solution)/shard_map/images/pallas_call | solution.py:376
  30.3 12.8 %all_to_all.17 = f32[32,1,128]{2,1,0:T(1,128)S(1)} all-to-all(f32[32,1,128]{2,1,0:T(1,128)S(1)} %bitcast.11), channel_id=1, replica_groups=mesh['scan'=8,'quad'=4,'place'=4] {'scan','quad'}, dimensions={0} | all-to-all | bytes 32768 | tf_op jit(solution)/shard_map/all_to_all | solution.py:393
  43.1 0.8 %last.1 = (f32[8,512]{1,0:T(8,128)}, f32[8,512]{1,0:T(8,128)}) custom-call(f32[32,128]{1,0:T(8,128)S(1)} %bitcast.10, f32[9,8,128]{2,1,0:T(8,128)S(1)} %combine.1.own_ref.fields_ref, f32[8,8,128]{2,1,0:T(8,128)S(1)} %get-tuple-element.10.first_ref, f32[8,8,128]{2,1,0:T(8,128)S(1)} %get-tuple-element.11.second_ref), custom_call_target="tpu_custom_call" | custom-call | tf_op jit(solution)/shard_map/last/pallas_call | solution.py:394
Async XLA Ops:
  2.2 11.1 %copy-start.1 = (s32[8,27]{1,0:T(8,128)S(1)}, s32[8,27]{1,0:T(8,128)}, u32[]{:S(2)}) copy-start(s32[8,27]{1,0:T(8,128)} %near_ref.1) | copy-start | bytes 2596
  13.3 14.2 %copy-start = (bf16[512,128]{1,0:T(8,128)(2,1)S(1)}, bf16[512,128]{1,0:T(8,128)(2,1)}, u32[]{:S(2)}) copy-start(bf16[512,128]{1,0:T(8,128)(2,1)} %constant.2.clone.table_ref) | copy-start | bytes 393220
  13.5 4.4 %collective-permute-start = (f32[9,8,128]{2,1,0:T(8,128)S(1)}, f32[9,8,128]{2,1,0:T(8,128)S(1)}, u32[]{:S(2)}, u32[]{:S(2)}) collective-permute-start(f32[9,8,128]{2,1,0:T(8,128)S(1)} %combine.1.own_ref.fields_ref), channel_id=1, source_target_pairs={{0,124},{1,125},{2,6},{3,7},{4,0},{5,1},{6,10},{7,11},{8,4},{9,5},... | collective-permute-start | bytes 110600 | tf_op jit(solution)/shard_map/ppermute | solution.py:364
  17.9 9.6 %collective-permute-start.2 = (f32[18,8,128]{2,1,0:T(8,128)S(1)}, f32[18,8,128]{2,1,0:T(8,128)S(1)}, u32[]{:S(2)}, u32[]{:S(2)}) collective-permute-start(f32[18,8,128]{2,1,0:T(8,128)S(1)} %get-tuple-element.8), channel_id=1, source_target_pairs={{0,2},{1,3},{2,0},{3,1},{4,6},{5,7},{6,4},{7,5},{8,10},{9,11},{10,... | collective-permute-start | bytes 221192 | tf_op jit(solution)/shard_map/ppermute | solution.py:373
  22.4 5.1 %collective-permute-start.3 = (f32[17,8,128]{2,1,0:T(8,128)S(1)}, f32[17,8,128]{2,1,0:T(8,128)S(1)}, u32[]{:S(2)}, u32[]{:S(2)}) collective-permute-start(f32[17,8,128]{2,1,0:T(8,128)S(1)} %get-tuple-element.7.own_ref), channel_id=1, source_target_pairs={{0,3},{1,2},{2,1},{3,0},{4,7},{5,6},{6,5},{7,4},{8,11},{9,10},{10,... | collective-permute-start | bytes 208904 | tf_op jit(solution)/shard_map/ppermute | solution.py:373
  22.7 4.8 %collective-permute-start.1 = (f32[17,8,128]{2,1,0:T(8,128)S(1)}, f32[17,8,128]{2,1,0:T(8,128)S(1)}, u32[]{:S(2)}, u32[]{:S(2)}) collective-permute-start(f32[17,8,128]{2,1,0:T(8,128)S(1)} %get-tuple-element.7.own_ref), channel_id=1, source_target_pairs={{0,1},{1,0},{2,3},{3,2},{4,5},{5,4},{6,7},{7,6},{8,9},{9,8},{10,11... | collective-permute-start | bytes 208904 | tf_op jit(solution)/shard_map/ppermute | solution.py:373

commit v8 on v7

--- a/solution.py
+++ b/solution.py
@@ -10,7 +10,7 @@
 SCREEN = 16.0
 BLOCKS = 8
 SLOTS = 4
-SHARE = SLOTS * 8 + 1
+SHARE = SLOTS * 9
 ROOM = SLOTS * 8 + 8
 ALL = ("scan", "quad", "place")
 WINDOW = 8 * BLOCKS
@@ -100,14 +100,8 @@
         work_ref[pl.ds(place, 8), :] = jnp.where(first_half, total[:8], total[8:])
         block = (target % BLOCKS).astype(jnp.float32)
         work_ref[pl.ds(row * ROOM + SLOTS * 8 + slot, 1), :] = jnp.full((1, 128), block, jnp.float32)
-    group = lax.broadcasted_iota(jnp.int32, (1, 128), 1) // 32
     for row in range(8):
-        at = row * ROOM + SLOTS * 8
-        out_ref[row * SHARE : row * SHARE + SLOTS * 8, :] = work_ref[row * ROOM : at, :]
-        names = work_ref[at : at + 1, :]
-        for slot in range(1, SLOTS):
-            names = jnp.where(group == slot, work_ref[at + slot : at + slot + 1, :], names)
-        out_ref[row * SHARE + SLOTS * 8 : (row + 1) * SHARE, :] = names
+        out_ref[row * SHARE : (row + 1) * SHARE, :] = work_ref[row * ROOM : row * ROOM + SHARE, :]
 
 
 def local_names(table, base):
@@ -128,7 +122,7 @@
         names = parts_ref[at + SLOTS * 8 : at + SHARE, :]
         for slot in range(SLOTS):
             part = parts_ref[at + slot * 8 : at + slot * 8 + 8, :]
-            name = jnp.broadcast_to(names[:, 32 * slot : 32 * slot + 1], (8, 128))
+            name = jnp.broadcast_to(names[slot : slot + 1, :], (8, 128))
             for block in range(BLOCKS):
                 sums[block] = sums[block] + jnp.where(name == float(block), part, 0.0)
     for block in range(BLOCKS):

time: 44.1 us -> 44.1 us (level)
  no operation moved by 1% of the time
where the time goes in v8:
time: 44.1 us; the launch traced here: 43.8 us
  blocking collectives  24 us (54%)
  starting transfers between devices  8.56 us (19%)
  waiting for transfers between devices  5.4 us (12%)
  Pallas kernels  5.23 us (12%)
  between operations  0.67 us (2%)
    all_to_all x1, blocking collectives, per_device(): sums = resident(lax.all_to_all(sums, ('scan', 'quad'), 0, 0, tiled=True))  12.8 us
    all_to_all x1, blocking collectives, per_device(): lax.all_to_all(parts.reshape(8, 1, SHARE * 128), 'scan', 0, 0, tiled=True)  11.2 us
    ppermute x3, starting transfers between devices, per_device(): lax.ppermute(longer if step == 2 else packed, 'place', [(i, i ^ step) for...  5.24 us
    ppermute x3, waiting for transfers between devices, per_device(): lax.ppermute(longer if step == 2 else packed, 'place', [(i, i ^ step) for...  4.34 us
    ppermute x1, starting transfers between devices, per_device(): lax.ppermute(fields, ALL, [(i, (i - 4 if i % 4 < 2 else i + 4) % count) f...  3.32 us
    pallas_call x1, Pallas kernels, per_device(): pl.pallas_call(image_kernel, out_shape=(shape(BLOCKS, 8, 128), shape(BLOC...  2.74 us
    pallas_call x1, Pallas kernels, per_device(): pl.pallas_call(splat_kernel, out_shape=shape(8 * SHARE, 128), in_specs=sm...  1.53 us
    ppermute x1, waiting for transfers between devices, per_device(): lax.ppermute(fields, ALL, [(i, (i - 4 if i % 4 < 2 else i + 4) % count) f...  1.06 us
  transfers between devices with their start and end apart: 4, of which 2 were waited for; matrix products, arithmetic and copies ran while one was open for 0% of the time, Pallas kernels for 0%

profile of v8, /device:TPU:1, one launch (start us, length us, event | category | flops | bytes accessed | tf_op | source)
XLA Modules:
  0.0 43.8 jit_solution(6554172325611923496)
XLA Ops:
  0.6 1.5 %splat.1 = f32[288,128]{1,0:T(8,128)S(1)} custom-call(s32[16]{0:T(128)} %target_ref.1, f32[3,16,128]{2,1,0:T(8,128)} %bitcast.12, f32[3,16,128]{2,1,0:T(8,128)} %bitcast.13, f32[16,128]{1,0:T(8,128)} %weights_ref.1), custom_call_target="tpu_custom_call" | custom-call | tf_op jit(solution)/shard_map/splat/pallas_call | solution.py:338
  2.2 0.0 copy-start.1
  2.2 11.2 %all_to_all.16 = f32[8,1,4608]{2,1,0:T(1,128)S(1)} all-to-all(f32[8,1,4608]{2,1,0:T(1,128)S(1)} %bitcast.9), channel_id=1, replica_groups=mesh['scan'=8,'quad'=4,'place'=4] {'scan'}, dimensions={0} | all-to-all | bytes 294912 | tf_op jit(solution)/shard_map/all_to_all | solution.py:346
  13.4 0.0 copy-done.1
  13.4 0.0 copy-start
  13.4 0.1 combine.1.own_ref.fields_ref
  13.5 3.3 %collective-permute-start = (f32[9,8,128]{2,1,0:T(8,128)S(1)}, f32[9,8,128]{2,1,0:T(8,128)S(1)}, u32[]{:S(2)}, u32[]{:S(2)}) collective-permute-start(f32[9,8,128]{2,1,0:T(8,128)S(1)} %combine.1.own_ref.fields_ref), channel_id=1, source_target_pairs={{0,124},{1,125},{2,6},{3,7},{4,0},{5,1},{6,10},{7,11},{8,4},{9,5},... | collective-permute-start | bytes 110600 | tf_op jit(solution)/shard_map/ppermute | solution.py:358
  16.8 1.1 %collective-permute-done.beside_ref = f32[9,8,128]{2,1,0:T(8,128)S(1)} collective-permute-done((f32[9,8,128]{2,1,0:T(8,128)S(1)}, f32[9,8,128]{2,1,0:T(8,128)S(1)}, u32[]{:S(2)}, u32[]{:S(2)}) %collective-permute-start) | collective-permute-done | bytes 36896 | tf_op jit(solution)/shard_map/ppermute | solution.py:358
  17.9 0.1 pack.1
  18.0 4.5 %collective-permute-start.2 = (f32[18,8,128]{2,1,0:T(8,128)S(1)}, f32[18,8,128]{2,1,0:T(8,128)S(1)}, u32[]{:S(2)}, u32[]{:S(2)}) collective-permute-start(f32[18,8,128]{2,1,0:T(8,128)S(1)} %get-tuple-element.8), channel_id=1, source_target_pairs={{0,2},{1,3},{2,0},{3,1},{4,6},{5,7},{6,4},{7,5},{8,10},{9,11},{10,... | collective-permute-start | bytes 221192 | tf_op jit(solution)/shard_map/ppermute | solution.py:367
  22.5 0.3 collective-permute-start.3
  22.7 0.5 %collective-permute-start.1 = (f32[17,8,128]{2,1,0:T(8,128)S(1)}, f32[17,8,128]{2,1,0:T(8,128)S(1)}, u32[]{:S(2)}, u32[]{:S(2)}) collective-permute-start(f32[17,8,128]{2,1,0:T(8,128)S(1)} %get-tuple-element.7.own_ref), channel_id=1, source_target_pairs={{0,1},{1,0},{2,3},{3,2},{4,5},{5,4},{6,7},{7,6},{8,9},{9,8},{10,11... | collective-permute-start | bytes 208904 | tf_op jit(solution)/shard_map/ppermute | solution.py:367
  23.2 4.3 %collective-permute-done.3.three_ref = f32[17,8,128]{2,1,0:T(8,128)S(1)} collective-permute-done((f32[17,8,128]{2,1,0:T(8,128)S(1)}, f32[17,8,128]{2,1,0:T(8,128)S(1)}, u32[]{:S(2)}, u32[]{:S(2)}) %collective-permute-start.3) | collective-permute-done | bytes 69664 | tf_op jit(solution)/shard_map/ppermute | solution.py:367
  27.5 0.0 collective-permute-done.1.one_ref
  27.5 0.0 collective-permute-done.2.two_ref
  27.5 0.0 copy-done
  27.5 2.7 %images.1 = (f32[8,8,128]{2,1,0:T(8,128)S(1)}, f32[8,8,128]{2,1,0:T(8,128)S(1)}, f32[32,128]{1,0:T(8,128)S(1)}) custom-call(f32[17,8,128]{2,1,0:T(8,128)S(1)} %get-tuple-element.7.own_ref, f32[17,8,128]{2,1,0:T(8,128)S(1)} %collective-permute-done.1.one_ref, f32[18,8,128]{2,1,0:T(8,128)S(1)} %collective-permute-done.2.two_ref, ...), custom_call_target="tpu_custom_call" | custom-call | tf_op jit(solution)/shard_map/images/pallas_call | solution.py:370
  30.3 12.8 %all_to_all.17 = f32[32,1,128]{2,1,0:T(1,128)S(1)} all-to-all(f32[32,1,128]{2,1,0:T(1,128)S(1)} %bitcast.11), channel_id=1, replica_groups=mesh['scan'=8,'quad'=4,'place'=4] {'scan','quad'}, dimensions={0} | all-to-all | bytes 32768 | tf_op jit(solution)/shard_map/all_to_all | solution.py:387
  43.1 0.8 %last.1 = (f32[8,512]{1,0:T(8,128)}, f32[8,512]{1,0:T(8,128)}) custom-call(f32[32,128]{1,0:T(8,128)S(1)} %bitcast.10, f32[9,8,128]{2,1,0:T(8,128)S(1)} %combine.1.own_ref.fields_ref, f32[8,8,128]{2,1,0:T(8,128)S(1)} %get-tuple-element.10.first_ref, f32[8,8,128]{2,1,0:T(8,128)S(1)} %get-tuple-element.11.second_ref), custom_call_target="tpu_custom_call" | custom-call | tf_op jit(solution)/shard_map/last/pallas_call | solution.py:388
Async XLA Ops:
  2.2 11.2 %copy-start.1 = (s32[8,27]{1,0:T(8,128)S(1)}, s32[8,27]{1,0:T(8,128)}, u32[]{:S(2)}) copy-start(s32[8,27]{1,0:T(8,128)} %near_ref.1) | copy-start | bytes 2596
  13.4 14.2 %copy-start = (bf16[512,128]{1,0:T(8,128)(2,1)S(1)}, bf16[512,128]{1,0:T(8,128)(2,1)}, u32[]{:S(2)}) copy-start(bf16[512,128]{1,0:T(8,128)(2,1)} %constant.2.clone.table_ref) | copy-start | bytes 393220
  13.5 4.4 %collective-permute-start = (f32[9,8,128]{2,1,0:T(8,128)S(1)}, f32[9,8,128]{2,1,0:T(8,128)S(1)}, u32[]{:S(2)}, u32[]{:S(2)}) collective-permute-start(f32[9,8,128]{2,1,0:T(8,128)S(1)} %combine.1.own_ref.fields_ref), channel_id=1, source_target_pairs={{0,124},{1,125},{2,6},{3,7},{4,0},{5,1},{6,10},{7,11},{8,4},{9,5},... | collective-permute-start | bytes 110600 | tf_op jit(solution)/shard_map/ppermute | solution.py:358
  18.0 9.6 %collective-permute-start.2 = (f32[18,8,128]{2,1,0:T(8,128)S(1)}, f32[18,8,128]{2,1,0:T(8,128)S(1)}, u32[]{:S(2)}, u32[]{:S(2)}) collective-permute-start(f32[18,8,128]{2,1,0:T(8,128)S(1)} %get-tuple-element.8), channel_id=1, source_target_pairs={{0,2},{1,3},{2,0},{3,1},{4,6},{5,7},{6,4},{7,5},{8,10},{9,11},{10,... | collective-permute-start | bytes 221192 | tf_op jit(solution)/shard_map/ppermute | solution.py:367
  22.5 5.1 %collective-permute-start.3 = (f32[17,8,128]{2,1,0:T(8,128)S(1)}, f32[17,8,128]{2,1,0:T(8,128)S(1)}, u32[]{:S(2)}, u32[]{:S(2)}) collective-permute-start(f32[17,8,128]{2,1,0:T(8,128)S(1)} %get-tuple-element.7.own_ref), channel_id=1, source_target_pairs={{0,3},{1,2},{2,1},{3,0},{4,7},{5,6},{6,5},{7,4},{8,11},{9,10},{10,... | collective-permute-start | bytes 208904 | tf_op jit(solution)/shard_map/ppermute | solution.py:367
  22.7 4.8 %collective-permute-start.1 = (f32[17,8,128]{2,1,0:T(8,128)S(1)}, f32[17,8,128]{2,1,0:T(8,128)S(1)}, u32[]{:S(2)}, u32[]{:S(2)}) collective-permute-start(f32[17,8,128]{2,1,0:T(8,128)S(1)} %get-tuple-element.7.own_ref), channel_id=1, source_target_pairs={{0,1},{1,0},{2,3},{3,2},{4,5},{5,4},{6,7},{7,6},{8,9},{9,8},{10,11... | collective-permute-start | bytes 208904 | tf_op jit(solution)/shard_map/ppermute | solution.py:367
